TPU v7x, 256 devices: a whole 4x4x8 slice. The times are simulated.
256 devices in a mesh: seq: 32 (over y, x, core), dp: 8 (over z).
Axes of the slice: x: 4, y: 4, z: 8, core: 2. Of those that a mesh axis runs over, the one named last changes fastest.
Arguments:
- saved: bfloat16 [2, 64, 4096, 768], P(None, 'dp', 'seq'), may hold values from -6 to 6
- cotangent: bfloat16 [64, 4096, 768], P('dp', 'seq'), may hold values from -6 to 6
- gain: float32 [2, 768], replicated, may hold values from 0.25 to 1.75
- weight: bfloat16 [2, 768, 3, 768], replicated, may hold values from -0.125 to 0.125
Outputs:
- grad_input: bfloat16 [64, 4096, 768], P('dp', 'seq')
- grad_weight: float32 [2, 768, 3, 768], P(None, 'seq', None, 'dp')
- grad_stats: float32 [2, 2, 768], replicated
All inputs are finite; a program needn't handle non-finite values.
Results may differ from a plain program's by a relative error of at most 0.0045.
Values may be sent and summed in bfloat16 or wider, within the bound.
A program may use at most 128 MiB of HBM per device.

v0:
```python
import math

import jax
import jax.numpy as jnp
from jax import lax
from jax.sharding import PartitionSpec as P

CONV_LAYERS = 2
BASE_DILATION = 16


EPS = 1e-06


def extended(cells, sides, width):
    for axis, dim in sides:
        count = lax.axis_size(axis)
        ends = count - 1
        head = lax.slice_in_dim(cells, 0, width, axis=dim)
        tail = lax.slice_in_dim(cells, cells.shape[dim] - width, cells.shape[dim], axis=dim)
        cells = jnp.concatenate(
            [
                lax.ppermute(tail, axis, [(i, (i + 1) % count) for i in range(ends)]),
                cells,
                lax.ppermute(head, axis, [((i + 1) % count, i) for i in range(ends)]),
            ],
            axis=dim,
        )
    return cells


def front_map(features, gain_row):
    mean_sq = jnp.mean(features * features, axis=-1, keepdims=True)
    normed = features * lax.rsqrt(mean_sq + EPS)
    return jax.nn.gelu(normed * gain_row)


def local(saved, cotangent, gain, weight):
    windows_here, bins_here, wide = cotangent.shape
    scaling = 1.0 / math.sqrt(windows_here * lax.axis_size("dp") * bins_here * lax.axis_size("seq"))
    wave_fronts = []
    pulls = []
    for section_index in range(CONV_LAYERS):
        act_f, backward_pull = jax.vjp(
            front_map, saved[section_index].astype(jnp.float32), gain[section_index]
        )
        wave_fronts.append(act_f.astype(jnp.bfloat16))
        pulls.append(backward_pull)
    running = cotangent.astype(jnp.float32)
    weight_list = [None] * CONV_LAYERS
    gain_list = [None] * CONV_LAYERS
    bias_list = [None] * CONV_LAYERS
    for section_index in reversed(range(CONV_LAYERS)):
        tap_spacing = BASE_DILATION * 2**section_index
        cot_bf = running.astype(jnp.bfloat16)
        both_halo = extended(
            jnp.stack([wave_fronts[section_index], cot_bf]), (("seq", 2),), tap_spacing
        )
        act_halo = both_halo[0]
        cot_halo = both_halo[1]
        cot_flat = cot_bf.reshape(-1, wide)
        act_taps = [
            act_halo[:, tap * tap_spacing : tap * tap_spacing + bins_here].reshape(-1, wide)
            for tap in range(3)
        ]
        blocks = [
            jnp.dot(tap_rows.T, cot_flat, preferred_element_type=jnp.float32)
            for tap_rows in act_taps
        ]
        row_owned = lax.psum_scatter(
            jnp.stack(blocks, axis=1) * scaling, "seq", scatter_dimension=0, tiled=True
        )
        weight_list[section_index] = lax.psum_scatter(
            row_owned, "dp", scatter_dimension=2, tiled=True
        )
        cot_taps = jnp.stack(
            [
                cot_halo[:, (2 - tap) * tap_spacing : (2 - tap) * tap_spacing + bins_here]
                for tap in range(3)
            ],
            axis=2,
        )
        cot_taps = cot_taps.reshape(-1, 3, wide)
        grad_act = lax.dot_general(
            cot_taps,
            weight[section_index],
            (((1, 2), (1, 2)), ((), ())),
            preferred_element_type=jnp.float32,
        )
        grad_feat, grad_gain = pulls[section_index](grad_act.reshape(windows_here, bins_here, wide))
        running = running + grad_feat
        gain_list[section_index] = grad_gain
        bias_list[section_index] = jnp.sum(cot_flat.astype(jnp.float32), axis=0)
    local_stats = jnp.stack([jnp.stack(gain_list), jnp.stack(bias_list)])
    grad_stats = lax.psum(local_stats, ("seq", "dp")) * scaling
    return (running.astype(jnp.bfloat16), jnp.stack(weight_list), grad_stats)


def solution(mesh):
    return jax.shard_map(
        local,
        mesh=mesh,
        in_specs=(P(None, "dp", "seq", None), P("dp", "seq", None), P(), P()),
        out_specs=(P("dp", "seq", None), P(None, "seq", None, "dp"), P()),
        check_vma=False,
    )
```

profile of v0, /device:TPU:1, one launch (start us, length us, event | category | flops | bytes accessed | tf_op | source)
XLA Modules:
  0.0 328.0 jit_solution(12526614593921514871)
XLA Ops:
  8.1 1.8 fusion.42
  9.9 2.8 fusion.47
  12.7 4.5 %collective-permute-start = (bf16[2,8,32,768]{3,2,1,0:T(8,128)(2,1)S(1)}, bf16[2,8,32,768]{3,2,1,0:T(8,128)(2,1)S(1)}, u32[]{:S(2)}, u32[]{:S(2)}) collective-permute-start(bf16[2,8,32,768]{3,2,1,0:T(8,128)(2,1)S(1)} %get-tuple-element.18), channel_id=1, source_target_pairs={{0,8},{8,16},{16,24},{24,32},{32,40},{40,48},{48,56},{56,64},{64,7... | collective-permute-start | bytes 2359304 | tf_op jit(solution)/shard_map/ppermute | solution.py:23
  17.3 2.0 collective-permute-start.1
  19.3 6.9 %collective-permute-done = bf16[2,8,32,768]{3,2,1,0:T(8,128)(2,1)S(1)} collective-permute-done((bf16[2,8,32,768]{3,2,1,0:T(8,128)(2,1)S(1)}, bf16[2,8,32,768]{3,2,1,0:T(8,128)(2,1)S(1)}, u32[]{:S(2)}, u32[]{:S(2)}) %collective-permute-start) | collective-permute-done | bytes 786464 | tf_op jit(solution)/shard_map/ppermute | solution.py:23
  26.2 4.4 %collective-permute-done.1 = bf16[2,8,32,768]{3,2,1,0:T(8,128)(2,1)S(1)} collective-permute-done((bf16[2,8,32,768]{3,2,1,0:T(8,128)(2,1)S(1)}, bf16[2,8,32,768]{3,2,1,0:T(8,128)(2,1)S(1)}, u32[]{:S(2)}, u32[]{:S(2)}) %collective-permute-start.1) | collective-permute-done | bytes 786464 | tf_op jit(solution)/shard_map/ppermute | solution.py:25
  30.9 1.8 slice_bitcast_fusion
  37.1 3.1 maximum_multiply_fusion.1
  40.5 2.8 slice_bitcast_fusion.9
  43.8 7.9 %fusion.41 = (f32[768]{0:T(1024)S(1)}, f32[8,128]{1,0:T(8,128)S(1)}, f32[8,128]{1,0:T(8,128)S(1)}, f32[8,128,768]{2,1,0:T(8,128)S(1)}) fusion(f32[8,128]{1,0:T(8,128)S(1)} %fusion.89, bf16[2,8,128,768]{3,2,1,0:T(8,128)(2,1)S(1)} %copy-done, f32[768]{0:T(1024)S(1)} %get-tuple-element.9, bf16[2,768,3,768]{3,1,2,0:T(8,128)(2,1)} %param.7, ...), kind=kOutput, calls=%fused_computation.59 | convolution fusion | flops 3652187392 | bytes 14567424 | tf_op jit(solution)/shard_map/dot_general | solution.py:84
  55.5 1.9 collective-permute-start.2
  57.5 2.6 collective-permute-start.3
  60.1 2.0 collective-permute-done.2
  62.2 4.4 %collective-permute-done.3 = bf16[2,8,16,768]{3,2,1,0:T(8,128)(2,1)S(1)} collective-permute-done((bf16[2,8,16,768]{3,2,1,0:T(8,128)(2,1)S(1)}, bf16[2,8,16,768]{3,2,1,0:T(8,128)(2,1)S(1)}, u32[]{:S(2)}, u32[]{:S(2)}) %collective-permute-start.3) | collective-permute-done | bytes 393248 | tf_op jit(solution)/shard_map/ppermute | solution.py:25
  72.8 3.2 maximum_multiply_fusion
  76.1 2.9 slice_bitcast_fusion.6
  79.0 9.4 %fusion.36 = (f32[768]{0:T(1024)S(1)}, f32[8,128]{1,0:T(8,128)S(1)}, f32[8,128,768]{2,1,0:T(8,128)}) fusion(f32[8,128]{1,0:T(8,128)S(1)} %get-tuple-element.31, bf16[2,8,128,768]{3,2,1,0:T(8,128)(2,1)S(1)} %copy-done, f32[768]{0:T(1024)S(1)} %get-tuple-element.8, bf16[2,768,3,768]{3,1,2,0:T(8,128)(2,1)} %param.7, ...), kind=kOutput, calls=%fused_computation.54 | convolution fusion | flops 3649829120 | bytes 12990464 | tf_op jit(solution)/shard_map/dot_general | solution.py:84
  88.4 50.2 %reduce-scatter.11.cloned.1.call-done = f32[24,3,768]{2,0,1:T(8,128)} async-done(((f32[768,3,768]{2,0,1:T(8,128)}), f32[24,3,768]{2,0,1:T(8,128)}) %reduce-scatter.11.cloned.1.call-update) | async-done | bytes 221200 | tf_op jit(solution)/shard_map/reduce_scatter | solution.py:70
  138.6 2.3 copy.36
  140.9 2.5 reshape.104
  143.8 5.2 %convert_reduce_fusion = (f32[768]{0:T(1024)S(1)}, bf16[8,128,768]{2,1,0:T(8,128)(2,1)}) fusion(bf16[8,128,768]{2,1,0:T(8,128)(2,1)} %param.5, f32[8,128]{1,0:T(8,128)S(1)} %multiply_multiply_fusion.6, bf16[2,8,128,768]{3,2,1,0:T(8,128)(2,1)S(1)} %copy-done, f32[8,128]{1,0:T(8,128)S(1)} %get-tuple-element.31, f32[8,128,768]{2,1,0:T(8,128)} %get-tuple-element.29, ...), kind=kLoop, calls=%fused_computation.36 | loop fusion | flops 13368576 | bytes 12608512 | tf_op jit(solution)/shard_map/reduce_sum | solution.py:93
  149.0 88.5 %reduce-scatter.9.cloned.1.call-done = f32[24,3,768]{2,0,1:T(8,128)} async-done(((f32[768,3,768]{2,0,1:T(8,128)}), f32[24,3,768]{2,0,1:T(8,128)}) %reduce-scatter.9.cloned.1.call-update) | async-done | bytes 221200 | tf_op jit(solution)/shard_map/reduce_scatter | solution.py:70
  237.6 1.6 copy.34
  240.5 77.7 %psum.7 = f32[2,2,768]{2,1,0:T(2,128)S(1)} all-reduce(f32[2,2,768]{2,1,0:T(2,128)S(1)} %pad_maximum_fusion.7), channel_id=1, replica_groups=mesh['seq'=32,'dp'=8] {'seq','dp'}, use_global_device_ids=true, to_apply=%region_12.0 | all-reduce | flops 3072 | bytes 24576 | tf_op jit(solution)/shard_map/psum | solution.py:95
  (49 shorter events, 21.5 us)
Async XLA Ops:
  7.2 5.5 %copy-start.1 = (bf16[8,128,768]{2,1,0:T(8,128)(2,1)S(1)}, bf16[8,128,768]{2,1,0:T(8,128)(2,1)}, u32[]{:S(2)}) copy-start(bf16[8,128,768]{2,1,0:T(8,128)(2,1)} %param.5) | copy-start | bytes 4718596
  7.2 131.4 %reduce-scatter.11.cloned.1.call-start = ((), (), s32[]{:S(2)}) async-start(), calls=%async_computation.5 | async-start | bytes 7299072 | tf_op jit(solution)/shard_map/reduce_scatter | solution.py:70
  12.7 13.4 %collective-permute-start = (bf16[2,8,32,768]{3,2,1,0:T(8,128)(2,1)S(1)}, bf16[2,8,32,768]{3,2,1,0:T(8,128)(2,1)S(1)}, u32[]{:S(2)}, u32[]{:S(2)}) collective-permute-start(bf16[2,8,32,768]{3,2,1,0:T(8,128)(2,1)S(1)} %get-tuple-element.18), channel_id=1, source_target_pairs={{0,8},{8,16},{16,24},{24,32},{32,40},{40,48},{48,56},{56,64},{64,7... | collective-permute-start | bytes 2359304 | tf_op jit(solution)/shard_map/ppermute | solution.py:23
  17.3 13.3 %collective-permute-start.1 = (bf16[2,8,32,768]{3,2,1,0:T(8,128)(2,1)S(1)}, bf16[2,8,32,768]{3,2,1,0:T(8,128)(2,1)S(1)}, u32[]{:S(2)}, u32[]{:S(2)}) collective-permute-start(bf16[2,8,32,768]{3,2,1,0:T(8,128)(2,1)S(1)} %get-tuple-element.19), channel_id=1, source_target_pairs={{8,0},{16,8},{24,16},{32,24},{40,32},{48,40},{56,48},{64,56},{72,6... | collective-permute-start | bytes 2359304 | tf_op jit(solution)/shard_map/ppermute | solution.py:25
  40.2 197.3 %reduce-scatter.9.cloned.1.call-start = ((), (), s32[]{:S(2)}) async-start(), calls=%async_computation.4 | async-start | bytes 7299072 | tf_op jit(solution)/shard_map/reduce_scatter | solution.py:70
  40.5 3.3 %copy-start = (bf16[2,8,128,768]{3,2,1,0:T(8,128)(2,1)S(1)}, bf16[2,8,128,768]{3,2,1,0:T(8,128)(2,1)}, u32[]{:S(2)}) copy-start(bf16[2,8,128,768]{3,2,1,0:T(8,128)(2,1)} %param.4) | copy-start | bytes 9437188
  51.7 3.7 %copy-start.3 = (f32[8,128,768]{2,1,0:T(8,128)}, f32[8,128,768]{2,1,0:T(8,128)S(1)}, u32[]{:S(2)}) copy-start(f32[8,128,768]{2,1,0:T(8,128)S(1)} %get-tuple-element.28) | copy-start | bytes 9437188
  51.7 2.5 copy-start.2
  55.5 6.6 %collective-permute-start.2 = (bf16[2,8,16,768]{3,2,1,0:T(8,128)(2,1)S(1)}, bf16[2,8,16,768]{3,2,1,0:T(8,128)(2,1)S(1)}, u32[]{:S(2)}, u32[]{:S(2)}) collective-permute-start(bf16[2,8,16,768]{3,2,1,0:T(8,128)(2,1)S(1)} %get-tuple-element.16), channel_id=1, source_target_pairs={{0,8},{8,16},{16,24},{24,32},{32,40},{40,48},{48,56},{56,64},{64,7... | collective-permute-start | bytes 1179656 | tf_op jit(solution)/shard_map/ppermute | solution.py:23
  57.5 9.1 %collective-permute-start.3 = (bf16[2,8,16,768]{3,2,1,0:T(8,128)(2,1)S(1)}, bf16[2,8,16,768]{3,2,1,0:T(8,128)(2,1)S(1)}, u32[]{:S(2)}, u32[]{:S(2)}) collective-permute-start(bf16[2,8,16,768]{3,2,1,0:T(8,128)(2,1)S(1)} %get-tuple-element.17), channel_id=1, source_target_pairs={{8,0},{16,8},{24,16},{32,24},{40,32},{48,40},{56,48},{64,56},{72,6... | collective-permute-start | bytes 1179656 | tf_op jit(solution)/shard_map/ppermute | solution.py:25
  76.0 242.8 %reduce-scatter.15.cloned.1.call-start = ((), (), s32[]{:S(2)}) async-start(), calls=%async_computation.7 | async-start | bytes 442368
  143.5 176.3 %reduce-scatter.13.cloned.1.call-start = ((), (), s32[]{:S(2)}) async-start(), calls=%async_computation.6 | async-start | bytes 442368
Sparse Core Ops, SparseCore 0:
  40.4 98.1 reduce-scatter.10
  142.7 94.8 reduce-scatter.8
  240.1 33.5 reduce-scatter.14
  276.2 35.7 reduce-scatter.12
where the time goes:
time: 329 us; the launch traced here: 328 us
  waiting for transfers between devices  157 us (48%)
  blocking collectives  77.7 us (24%)
  matrix products  26.1 us (8%)
  local copies, waits for them, and re-layouts  21.3 us (6%)
  other arithmetic  20.7 us (6%)
  between operations  14 us (4%)
  starting transfers between devices  11.7 us (4%)
    reduce_scatter x2, waiting for transfers between devices, local(): lax.psum_scatter(jnp.stack(blocks, axis=1) * scaling, 'seq', scatter_dime...  139 us
    psum x1, blocking collectives, local(): grad_stats = lax.psum(local_stats, ('seq', 'dp')) * scaling  77.7 us
    dot_general x2, matrix products, local(): lax.dot_general(cot_taps, weight[section_index], (((1, 2), (1, 2)), ((),...  17.3 us
    unnamed x16, local copies, waits for them, and re-layouts  11.4 us
    ppermute x2, waiting for transfers between devices, extended(): lax.ppermute(tail, axis, [(i, (i + 1) % count) for i in range(ends)])  8.97 us
    ppermute x2, waiting for transfers between devices, extended(): lax.ppermute(head, axis, [((i + 1) % count, i) for i in range(ends)])  8.79 us
    dot_general x6, matrix products, local(): jnp.dot(tap_rows.T, cot_flat, preferred_element_type=jnp.float32)  8.76 us
  transfers between devices with their start and end apart: 8, of which 6 were waited for; matrix products, arithmetic and copies ran while one was open for 15% of the time, Pallas kernels for 0%

commit v1 on v0

v1 whole, which is shorter than its diff:
```python
import functools
import math

import jax
import jax.numpy as jnp
from jax import lax
from jax.experimental import pallas as pl
from jax.experimental.pallas import tpu as pltpu
from jax.sharding import PartitionSpec as P

EPS = 1e-06
F32 = jnp.float32
BF16 = jnp.bfloat16
MESH = pl.DeviceIdType.MESH

C = 768
W = 8
B = 128
DIL = (16, 32)
NX, NY, NZ = 4, 4, 8
UNITS = 9
ROWS = 96
K0 = math.sqrt(2.0 / math.pi)
K1 = 0.044715
SCALE = 1.0 / math.sqrt(64 * 4096)


def body(
    saved, cot, gain, weight, gin, gw, gs,
    xv, wv, c0, c1, at, gp, rstd, run, gbuf, stage,
    csend, crecv, keep, rsend, rrecv, tbuf, ysend, yrecv, yown, zb, zs, zf, zr, zown,
    sacc, sa0, sa1, sa2, sa3,
    loc_sem, out_sem, halo_s, halo_r, c_s, c_r, r_s, r_r, y_s, y_r, z_s, z_r, st_s, st_r,
):
    seq = lax.axis_index("seq")
    z = lax.axis_index("dp")
    c = lax.rem(seq, 2)
    x = lax.rem(lax.div(seq, 2), NX)
    y = lax.div(seq, 2 * NX)
    cots = (c0, c1)

    def sid(yy, xx, cc):
        return (yy * NX + xx) * 2 + cc

    def rdma(src, dst, ssem, rsem, to_seq=None, to_z=None):
        where = {"seq": seq if to_seq is None else to_seq, "dp": z if to_z is None else to_z}
        return pltpu.make_async_remote_copy(
            src_ref=src, dst_ref=dst, send_sem=ssem, recv_sem=rsem, device_id=where, device_id_type=MESH
        )

    right = lax.rem(seq + 1, 32)
    left = lax.rem(seq + 31, 32)

    ld_x = [pltpu.make_async_copy(saved.at[l], xv.at[l], loc_sem.at[l]) for l in range(2)]
    ld_c = pltpu.make_async_copy(cot, c1.at[:, pl.ds(DIL[1], B), :], loc_sem.at[2])
    ld_w = [pltpu.make_async_copy(weight.at[l], wv.at[l], loc_sem.at[3 + l]) for l in range(2)]
    ld_x[1].start()
    ld_c.start()
    ld_w[1].start()
    ld_x[0].start()
    ld_w[0].start()

    bar = pltpu.get_barrier_semaphore()
    peers = [(sid(y, x, 1 - c), z), (lax.rem(seq + 2 * c + 31, 32), z)]
    peers += [(sid(y, lax.rem(x + o, NX), c), z) for o in range(1, NX)]
    peers += [(sid(lax.rem(y + o, NY), x, c), z) for o in range(1, NY)]
    peers += [(seq, lax.rem(z + o, NZ)) for o in range(1, NZ)]
    for s, zz in peers:
        pl.semaphore_signal(bar, inc=1, device_id={"seq": s, "dp": zz}, device_id_type=MESH)
    pl.semaphore_wait(bar, len(peers))

    def halo1():
        d = DIL[1]
        return (
            rdma(cot.at[:, pl.ds(0, d), :], c1.at[:, pl.ds(B + d, d), :], halo_s.at[0], halo_r.at[0], to_seq=left),
            rdma(cot.at[:, pl.ds(B - d, d), :], c1.at[:, pl.ds(0, d), :], halo_s.at[1], halo_r.at[1], to_seq=right),
        )

    def halo0(m):
        d = DIL[0]
        ws = pl.ds(2 * m, 2)
        return (
            rdma(c0.at[ws, pl.ds(d, d), :], c0.at[ws, pl.ds(B + d, d), :], halo_s.at[2 + 2 * m], halo_r.at[2 + 2 * m], to_seq=left),
            rdma(c0.at[ws, pl.ds(B, d), :], c0.at[ws, pl.ds(0, d), :], halo_s.at[3 + 2 * m], halo_r.at[3 + 2 * m], to_seq=right),
        )

    def clear_ends(l):
        d = DIL[l]
        zero = jnp.zeros((W, d, C), BF16)

        @pl.when(seq == 0)
        def _():
            cots[l][:, pl.ds(0, d), :] = zero

        @pl.when(seq == 31)
        def _():
            cots[l][:, pl.ds(B + d, d), :] = zero

    for h in halo1():
        h.start()

    def forward(l, w):
        xt = xv[l, w].astype(F32)
        g = gain[pl.ds(l, 1), :]
        inv = lax.rsqrt(jnp.mean(xt * xt, axis=-1, keepdims=True) + EPS)
        rstd[l, w] = jnp.broadcast_to(inv, (B, 128))
        u = xt * inv * g
        u2 = u * u
        t = jnp.tanh(u * (K0 + (K0 * K1) * u2))
        h = 0.5 + 0.5 * t
        act = u * h
        gp[l, w] = h + act * (1.0 - h) * (2.0 * K0 + (6.0 * K0 * K1) * u2)
        a = act.T
        cols = pl.ds(pl.multiple_of(w * B, B), B)
        for cc in range(2):
            for t_ in range(2):
                parts = []
                for dest in range(4):
                    for other in range(4):
                        yy, xx = (other, dest) if t_ == 0 else (dest, other)
                        r0 = sid(yy, xx, cc) * 24
                        parts.append(a[r0 : r0 + 24])
                at[l, t_, cc, :, cols] = jnp.concatenate(parts, axis=0).astype(BF16)

    def kind(l, u):
        return lax.rem(u + (1 - l), 2)

    def near(t, o):
        return jnp.where(t == 0, sid(y, lax.rem(x + o, NX), c), sid(lax.rem(y + o, NY), x, c))

    def far(t, o):
        return jnp.where(t == 0, sid(lax.rem(y + o, NY), x, c), sid(y, lax.rem(x + o, NX), c))

    def tap_of(u):
        return 2 - lax.rem(lax.div(u, 3) + 1, 3)

    def core_copy(l, u):
        return rdma(csend.at[l, u], crecv.at[l, u], c_s.at[l, u], c_r.at[l, u], to_seq=sid(y, x, 1 - c))

    def ring_copy(l, u, i):
        o = 1 if i in (0, 2, 4) else 3
        return rdma(rsend.at[l, u, i], rrecv.at[l, u, i], r_s.at[l, u, i], r_r.at[l, u, i], to_seq=near(kind(l, u), o))

    def far_copy(l, u, o):
        return rdma(ysend.at[l, u, o - 1], yrecv.at[l, u, o - 1], y_s.at[l, u, o - 1], y_r.at[l, u, o - 1], to_seq=far(kind(l, u), o))

    def z_copy(l, o):
        to = lax.rem(z + o, NZ)
        return rdma(zs.at[l, to], zr.at[l, o - 1], z_s.at[l, o - 1], z_r.at[l, o - 1], to_z=to)

    def stage_a(l, u):
        d = DIL[l]
        t = kind(l, u)
        off = pl.multiple_of(lax.rem(lax.div(u, 3) + 1, 3) * d, 16)
        n0 = pl.multiple_of(lax.rem(u, 3) * 256, 256)
        rhs = cots[l][:, pl.ds(off, B), pl.ds(n0, 256)].reshape(W * B, 256)
        csend[l, u] = jnp.dot(at[l, t, 1 - c], rhs, preferred_element_type=F32).astype(BF16)
        core_copy(l, u).start()
        keep[u] = jnp.dot(at[l, t, c], rhs, preferred_element_type=F32)

    def stage_b(l, u):
        t = kind(l, u)
        p = jnp.where(t == 0, x, y)
        core_copy(l, u).wait_recv()

        def rows(o, lo, n):
            return pl.ds(pl.multiple_of(lax.rem(p + o, 4) * ROWS + lo, 16), n)

        def total(o, lo, n):
            r = rows(o, lo, n)
            return keep[u, r, :] + crecv[l, u, r, :].astype(F32)

        rsend[l, u, 0] = total(2, 0, 48).astype(BF16)
        ring_copy(l, u, 0).start()
        rsend[l, u, 1] = total(2, 48, 48).astype(BF16)
        ring_copy(l, u, 1).start()
        rsend[l, u, 2] = total(1, 48, 48).astype(BF16)
        ring_copy(l, u, 2).start()
        rsend[l, u, 3] = total(3, 0, 48).astype(BF16)
        ring_copy(l, u, 3).start()
        keep[u, rows(1, 0, 48), :] = total(1, 0, 48)
        keep[u, rows(3, 48, 48), :] = total(3, 48, 48)
        keep[u, rows(0, 0, ROWS), :] = total(0, 0, ROWS)

    def stage_c(l, u):
        t = kind(l, u)
        p = jnp.where(t == 0, x, y)
        up = pl.ds(pl.multiple_of(lax.rem(p + 1, 4) * ROWS, 16), 48)
        down = pl.ds(pl.multiple_of(lax.rem(p + 3, 4) * ROWS + 48, 16), 48)
        ring_copy(l, u, 0).wait_recv()
        rsend[l, u, 4] = (keep[u, up, :] + rrecv[l, u, 0].astype(F32)).astype(BF16)
        ring_copy(l, u, 4).start()
        ring_copy(l, u, 1).wait_recv()
        rsend[l, u, 5] = (keep[u, down, :] + rrecv[l, u, 1].astype(F32)).astype(BF16)
        ring_copy(l, u, 5).start()

    def stage_d(l, u):
        t = kind(l, u)
        p = jnp.where(t == 0, x, y)
        q = jnp.where(t == 0, y, x)
        for i in (2, 3, 4, 5):
            ring_copy(l, u, i).wait_recv()
        r0 = pl.multiple_of(p * ROWS, 16)
        half0 = keep[u, pl.ds(r0, 48), :] + rrecv[l, u, 3].astype(F32) + rrecv[l, u, 4].astype(F32)
        half1 = keep[u, pl.ds(r0 + 48, 48), :] + rrecv[l, u, 2].astype(F32) + rrecv[l, u, 5].astype(F32)
        tbuf[pl.ds(0, 2)] = half0.reshape(2, 24, 256)
        tbuf[pl.ds(2, 2)] = half1.reshape(2, 24, 256)
        for o in (2, 1, 3):
            v = tbuf[lax.rem(q + o, 4)]
            ysend[l, u, o - 1] = jnp.concatenate([v[:, :128], v[:, 128:]], axis=0).astype(BF16)
            far_copy(l, u, o).start()
        yown[u] = tbuf[q]

    def stage_e(l, u):
        for o in (1, 3, 2):
            far_copy(l, u, o).wait_recv()
        n0 = pl.multiple_of(lax.rem(u, 3) * 256, 256)
        s = yrecv[l, u, 0].astype(F32) + yrecv[l, u, 1].astype(F32) + yrecv[l, u, 2].astype(F32)
        zb[tap_of(u), :, pl.ds(n0, 256)] = yown[u] + jnp.concatenate([s[:24], s[24:]], axis=1)

    def stage_z(l):
        v = zb[...].reshape(72, C)
        pad = jnp.zeros((8, 128), F32)
        for zz in range(NZ):
            part = v[:, zz * 96 : zz * 96 + 96]
            part = jnp.concatenate([part, jnp.zeros((72, 32), F32)], axis=1)
            zf[zz] = part
            zs[l, zz] = jnp.concatenate([part, pad], axis=0).astype(BF16)
        for o in (4, 3, 5, 2, 6, 1, 7):
            z_copy(l, o).start()
        zown[l] = zf[z]

    def stage_last(l):
        for o in (1, 7, 2, 6, 3, 5, 4):
            z_copy(l, o).wait_recv()
        tot = zown[l]
        for o in range(1, NZ):
            tot = tot + zr[l, o - 1].astype(F32)[:72]
        tot = (tot * SCALE).reshape(3, 24, 128)
        gw[l] = tot[:, :, :96]


    def matmul(l, m):
        d = DIL[l]
        for n in range(3):
            acc = None
            for k in range(3):
                lhs = cots[l][pl.ds(2 * m, 2), pl.ds((2 - k) * d, B), :].reshape(2 * B, C)
                part = lax.dot_general(
                    lhs, wv[l, k, n * 256 : n * 256 + 256, :], (((1,), (1,)), ((), ())), preferred_element_type=F32
                )
                acc = part if acc is None else acc + part
            gbuf[:, n * 256 : n * 256 + 256] = acc

    def backward(l, m):
        g = gain[pl.ds(l, 1), :]
        for half in range(2):
            w = 2 * m + half
            for q in range(2):
                r = pl.ds(q * 64, 64)
                ga = gbuf[half * 128 + q * 64 : half * 128 + q * 64 + 64, :]
                inv = rstd[l, w, r, :][:, :1]
                n = xv[l, w, r, :].astype(F32) * inv
                du = ga * gp[l, w, r, :]
                sacc[l] += (du * n).reshape(8, 8, C).sum(axis=0)
                dn = du * g
                mean = jnp.mean(dn * n, axis=-1, keepdims=True)
                dx = inv * (dn - n * mean)
                if l == 1:
                    ct = c1[w, pl.ds(DIL[1] + q * 64, 64), :].astype(F32)
                    sacc[3] += ct.reshape(8, 8, C).sum(axis=0)
                    new = ct + dx
                    run[w, r, :] = new
                    nb = new.astype(BF16)
                    c0[w, pl.ds(DIL[0] + q * 64, 64), :] = nb
                    sacc[2] += nb.astype(F32).reshape(8, 8, C).sum(axis=0)
                else:
                    stage[w, r, :] = (run[w, r, :] + dx).astype(BF16)

    def out_copy(m):
        ws = pl.ds(2 * m, 2)
        return pltpu.make_async_copy(stage.at[ws], gin.at[ws], out_sem.at[m])

    bufs = (sa0, sa1, sa2, sa3)
    places = (c, x, y, z)
    counts = (2, NX, NY, NZ)
    first = (0, 1, 4, 7)

    def stat_copy(e, ax, o, sending):
        n = counts[ax]
        slot = places[ax] if sending else lax.rem(places[ax] + n - o, n)
        lo, cnt = ((0, 1), (1, 3))[e]
        to = (
            dict(to_seq=sid(y, x, 1 - c)),
            dict(to_seq=sid(y, lax.rem(x + o, NX), c)),
            dict(to_seq=sid(lax.rem(y + o, NY), x, c)),
            dict(to_z=lax.rem(z + o, NZ)),
        )[ax]
        ref = bufs[ax].at[slot, pl.ds(lo, cnt)]
        i = first[ax] + o - 1
        return rdma(ref, ref, st_s.at[e, i], st_r.at[e, i], **to)

    def stat_put(e):
        for i in ((0,), (1, 2, 3))[e]:
            v = jnp.sum(sacc[i], axis=0, keepdims=True)
            sa0[c, i] = jnp.zeros((8, 128), F32)
            for j in range(6):
                sa0[c, i, j : j + 1, :] = v[:, j * 128 : j * 128 + 128]

    def stat_send(e, ax):
        for o in range(1, counts[ax]):
            stat_copy(e, ax, o, True).start()

    def stat_recv(e, ax):
        for o in range(1, counts[ax]):
            stat_copy(e, ax, o, False).wait_recv()
        lo, cnt = ((0, 1), (1, 3))[e]
        tot = bufs[ax][0, lo : lo + cnt]
        for i in range(1, counts[ax]):
            tot = tot + bufs[ax][i, lo : lo + cnt]
        if ax < 3:
            bufs[ax + 1][places[ax + 1], lo : lo + cnt] = tot
        else:
            tot = tot * SCALE
            for i in range(cnt):
                a, b = ((0, 0), (0, 1), (1, 0), (1, 1))[lo + i]
                for j in range(6):
                    gs[a, b : b + 1, j * 128 : j * 128 + 128] = tot[i, j : j + 1, :]

    sacc[...] = jnp.zeros_like(sacc)
    ld_x[1].wait()

    @pl.loop(0, W)
    def _(w):
        forward(1, w)

    ld_c.wait()

    def grad_weight(l, before):
        @pl.loop(0, UNITS)
        def _(u):
            @pl.when(u == 3)
            def _():
                before()

            stage_a(l, u)

            @pl.when(u >= 1)
            def _():
                stage_b(l, u - 1)

            @pl.when(u >= 3)
            def _():
                stage_c(l, u - 3)

        stage_b(l, UNITS - 1)

    def drain(l, m):
        @pl.loop(0, 3)
        def _(i):
            @pl.when(m == 0)
            def _():
                stage_c(l, 6 + i)

            @pl.when(m < 3)
            def _():
                stage_d(l, 3 * m + i)

            @pl.when(m >= 1)
            def _():
                stage_e(l, 3 * m - 3 + i)

    def halo1_in():
        for h in halo1():
            h.wait_recv()
        clear_ends(1)

    def halo0_in():
        for m in range(4):
            for h in halo0(m):
                h.wait_recv()
        clear_ends(0)

    grad_weight(1, halo1_in)
    ld_w[1].wait()

    @pl.loop(0, 4)
    def _(m):
        matmul(1, m)
        backward(1, m)
        for h in halo0(m):
            h.start()
        drain(1, m)

    stage_z(1)
    ld_x[0].wait()

    @pl.loop(0, W)
    def _(w):
        forward(0, w)

    stat_put(1)
    stat_send(1, 0)
    grad_weight(0, halo0_in)
    stat_recv(1, 0)
    stat_send(1, 1)
    stage_last(1)
    ld_w[0].wait()

    @pl.loop(0, 4)
    def _(m):
        matmul(0, m)
        backward(0, m)
        out_copy(m).start()
        drain(0, m)

    stat_recv(1, 1)
    stat_send(1, 2)
    stat_put(0)
    stat_send(0, 0)
    stage_z(0)
    stat_recv(1, 2)
    stat_send(1, 3)
    stat_recv(0, 0)
    stat_send(0, 1)
    stat_recv(0, 1)
    stat_send(0, 2)
    stat_recv(0, 2)
    stat_send(0, 3)
    stage_last(0)
    stat_recv(1, 3)
    stat_recv(0, 3)

    for h in halo1():
        h.wait_send()

    @pl.loop(0, 4)
    def _(m):
        out_copy(m).wait()
        for h in halo0(m):
            h.wait_send()

    for l in range(2):

        @pl.loop(0, UNITS)
        def _(u, l=l):
            core_copy(l, u).wait_send()
            for i in range(6):
                ring_copy(l, u, i).wait_send()
            for o in range(1, 4):
                far_copy(l, u, o).wait_send()

        for o in range(1, NZ):
            z_copy(l, o).wait_send()
    for e in range(2):
        for ax in range(4):
            for o in range(1, counts[ax]):
                stat_copy(e, ax, o, True).wait_send()


def local(saved, cotangent, gain, weight):
    wt = weight.transpose(0, 2, 1, 3)
    dma = pltpu.SemaphoreType.DMA
    vm = pltpu.VMEM
    scratch = dict(
        xv=vm((2, W, B, C), BF16),
        wv=vm((2, 3, C, C), BF16),
        c0=vm((W, B + 2 * DIL[0], C), BF16),
        c1=vm((W, B + 2 * DIL[1], C), BF16),
        at=vm((2, 2, 2, 384, W * B), BF16),
        gp=vm((2, W, B, C), F32),
        rstd=vm((2, W, B, 128), F32),
        run=vm((W, B, C), F32),
        gbuf=vm((2 * B, C), F32),
        stage=vm((W, B, C), BF16),
        csend=vm((2, UNITS, 384, 256), BF16),
        crecv=vm((2, UNITS, 384, 256), BF16),
        keep=vm((UNITS, 384, 256), F32),
        rsend=vm((2, UNITS, 6, 48, 256), BF16),
        rrecv=vm((2, UNITS, 6, 48, 256), BF16),
        tbuf=vm((4, 24, 256), F32),
        ysend=vm((2, UNITS, 3, 48, 128), BF16),
        yrecv=vm((2, UNITS, 3, 48, 128), BF16),
        yown=vm((UNITS, 24, 256), F32),
        zb=vm((3, 24, C), F32),
        zs=vm((2, NZ, 80, 128), BF16),
        zf=vm((NZ, 72, 128), F32),
        zr=vm((2, NZ - 1, 80, 128), BF16),
        zown=vm((2, 72, 128), F32),
        sacc=vm((4, 8, C), F32),
        sa0=vm((2, 4, 8, 128), F32),
        sa1=vm((NX, 4, 8, 128), F32),
        sa2=vm((NY, 4, 8, 128), F32),
        sa3=vm((NZ, 4, 8, 128), F32),
        loc_sem=dma((5,)),
        out_sem=dma((4,)),
        halo_s=dma((10,)),
        halo_r=dma((10,)),
        c_s=dma((2, UNITS)),
        c_r=dma((2, UNITS)),
        r_s=dma((2, UNITS, 6)),
        r_r=dma((2, UNITS, 6)),
        y_s=dma((2, UNITS, 3)),
        y_r=dma((2, UNITS, 3)),
        z_s=dma((2, NZ - 1)),
        z_r=dma((2, NZ - 1)),
        st_s=dma((2, 14)),
        st_r=dma((2, 14)),
    )
    names = list(scratch)

    def kernel(*refs):
        named = dict(zip(names, refs[7:]))
        body(*refs[:7], **named)

    gin, gw, gs = pl.pallas_call(
        kernel,
        out_shape=(
            jax.ShapeDtypeStruct((W, B, C), BF16),
            jax.ShapeDtypeStruct((2, 3, 24, 96), F32),
            jax.ShapeDtypeStruct((2, 2, C), F32),
        ),
        in_specs=[
            pl.BlockSpec(memory_space=pl.ANY),
            pl.BlockSpec(memory_space=pl.ANY),
            pl.BlockSpec(memory_space=pltpu.VMEM),
            pl.BlockSpec(memory_space=pl.ANY),
        ],
        out_specs=(
            pl.BlockSpec(memory_space=pl.ANY),
            pl.BlockSpec(memory_space=pltpu.VMEM),
            pl.BlockSpec(memory_space=pltpu.VMEM),
        ),
        scratch_shapes=list(scratch.values()),
        compiler_params=pltpu.CompilerParams(
            collective_id=0, has_side_effects=True, vmem_limit_bytes=62 * 1024 * 1024
        ),
        cost_estimate=pl.CostEstimate(flops=14_500_000_000, bytes_accessed=13_000_000, transcendentals=1_600_000),
    )(saved, cotangent, gain, wt)
    return gin, gw.transpose(0, 2, 1, 3), gs


def solution(mesh):
    return jax.shard_map(
        local,
        mesh=mesh,
        in_specs=(P(None, "dp", "seq", None), P("dp", "seq", None), P(), P()),
        out_specs=(P("dp", "seq", None), P(None, "seq", None, "dp"), P()),
        check_vma=False,
    )
```

time: 329 us -> 91.7 us (0.28)
  the two profiles are of different devices: /device:TPU:1 before, /device:TPU:2 now
where the time goes in v1:
time: 91.7 us; the launch traced here: 91.5 us
  Pallas kernels  87 us (95%)
  local copies, waits for them, and re-layouts  3.92 us (4%)
    pallas_call x1, Pallas kernels, local(): pl.pallas_call(kernel, out_shape=(jax.ShapeDtypeStruct((W, B, C), BF16),...  87 us
    unnamed x7, local copies, waits for them, and re-layouts  3.92 us

profile of v1, /device:TPU:2, one launch (start us, length us, event | category | flops | bytes accessed | tf_op | source)
XLA Modules:
  0.0 91.5 jit_solution(3038960318126557098)
XLA Ops:
  0.6 87.0 %shard_map.67 = (bf16[8,128,768]{2,1,0:T(8,128)(2,1)}, f32[2,3,24,96]{3,2,1,0:T(8,128)}, f32[2,2,768]{2,1,0:T(2,128)}) custom-call(bf16[2,8,128,768]{3,2,1,0:T(8,128)(2,1)} %refs_0_.1, bf16[8,128,768]{2,1,0:T(8,128)(2,1)} %refs_1_.1, f32[2,768]{1,0:T(2,128)} %refs_2_.1, bf16[2,3,768,768]{3,2,1,0:T(8,128)(2,1)} %bitcast.3), custom_call_target="tpu_custom_call" | custom-call | flops 14499999744 | bytes 13000000 | tf_op jit(solution)/shard_map/pallas_call | solution.py:516
  87.6 0.0 copy-start
  87.6 0.0 copy-start.1
  87.6 2.7 %copy.10 = bf16[8,128,768]{2,1,0:T(8,128)(2,1)} copy(bf16[8,128,768]{2,1,0:T(8,128)(2,1)} %get-tuple-element.12) | data formatting | bytes 3145728
  90.3 0.0 copy-done
  90.3 0.6 copy.11
  90.9 0.0 copy-done.1
  90.9 0.6 copy.12
Async XLA Ops:
  87.6 2.7 %copy-start = (f32[2,3,24,96]{3,2,1,0:T(8,128)S(1)}, f32[2,3,24,96]{3,2,1,0:T(8,128)}, u32[]{:S(2)}) copy-start(f32[2,3,24,96]{3,2,1,0:T(8,128)} %get-tuple-element.7) | copy-start | bytes 165892
  87.6 3.3 %copy-start.1 = (f32[2,2,768]{2,1,0:T(2,128)S(1)}, f32[2,2,768]{2,1,0:T(2,128)}, u32[]{:S(2)}) copy-start(f32[2,2,768]{2,1,0:T(2,128)} %get-tuple-element.14) | copy-start | bytes 36868

commit v2 on v1

--- a/solution.py
+++ b/solution.py
@@ -20,6 +20,8 @@
 NX, NY, NZ = 4, 4, 8
 UNITS = 9
 ROWS = 96
+TAPS = (1, 0, 2)
+RING = (False, True)
 K0 = math.sqrt(2.0 / math.pi)
 K1 = 0.044715
 SCALE = 1.0 / math.sqrt(64 * 4096)
@@ -28,8 +30,8 @@
 def body(
     saved, cot, gain, weight, gin, gw, gs,
     xv, wv, c0, c1, at, gp, rstd, run, gbuf, stage,
-    csend, crecv, keep, rsend, rrecv, tbuf, ysend, yrecv, yown, zb, zs, zf, zr, zown,
-    sacc, sa0, sa1, sa2, sa3,
+    csend, crecv, keep, rsend0, rrecv0, rsend1, rrecv1, tbuf, ysend, yrecv, yown, zb, zs, zf, zr, zown,
+    sacc, sa0, sa1, sa2,
     loc_sem, out_sem, halo_s, halo_r, c_s, c_r, r_s, r_r, y_s, y_r, z_s, z_r, st_s, st_r,
 ):
     seq = lax.axis_index("seq")
@@ -60,10 +62,12 @@
     ld_x[0].start()
     ld_w[0].start()
 
+    def plane(o):
+        return sid(lax.rem(y + o // NX, NY), lax.rem(x + o % NX, NX), c)
+
     bar = pltpu.get_barrier_semaphore()
     peers = [(sid(y, x, 1 - c), z), (lax.rem(seq + 2 * c + 31, 32), z)]
-    peers += [(sid(y, lax.rem(x + o, NX), c), z) for o in range(1, NX)]
-    peers += [(sid(lax.rem(y + o, NY), x, c), z) for o in range(1, NY)]
+    peers += [(plane(o), z) for o in range(1, NX * NY)]
     peers += [(seq, lax.rem(z + o, NZ)) for o in range(1, NZ)]
     for s, zz in peers:
         pl.semaphore_signal(bar, inc=1, device_id={"seq": s, "dp": zz}, device_id_type=MESH)
@@ -137,16 +141,20 @@
     def core_copy(l, u):
         return rdma(csend.at[l, u], crecv.at[l, u], c_s.at[l, u], c_r.at[l, u], to_seq=sid(y, x, 1 - c))
 
+    sends, recvs = (rsend0, rsend1), (rrecv0, rrecv1)
+
     def ring_copy(l, u, i):
-        o = 1 if i in (0, 2, 4) else 3
-        return rdma(rsend.at[l, u, i], rrecv.at[l, u, i], r_s.at[l, u, i], r_r.at[l, u, i], to_seq=near(kind(l, u), o))
+        o = (1 if i in (0, 2, 4) else 3) if RING[l] else i + 1
+        return rdma(
+            sends[l].at[u, i], recvs[l].at[u, i], r_s.at[l, u, i], r_r.at[l, u, i], to_seq=near(kind(l, u), o)
+        )
 
     def far_copy(l, u, o):
         return rdma(ysend.at[l, u, o - 1], yrecv.at[l, u, o - 1], y_s.at[l, u, o - 1], y_r.at[l, u, o - 1], to_seq=far(kind(l, u), o))
 
-    def z_copy(l, o):
+    def z_copy(l, g, o):
         to = lax.rem(z + o, NZ)
-        return rdma(zs.at[l, to], zr.at[l, o - 1], z_s.at[l, o - 1], z_r.at[l, o - 1], to_z=to)
+        return rdma(zs.at[l, g, to], zr.at[l, g, o - 1], z_s.at[l, g, o - 1], z_r.at[l, g, o - 1], to_z=to)
 
     def stage_a(l, u):
         d = DIL[l]
@@ -170,16 +178,16 @@
             r = rows(o, lo, n)
             return keep[u, r, :] + crecv[l, u, r, :].astype(F32)
 
-        rsend[l, u, 0] = total(2, 0, 48).astype(BF16)
-        ring_copy(l, u, 0).start()
-        rsend[l, u, 1] = total(2, 48, 48).astype(BF16)
-        ring_copy(l, u, 1).start()
-        rsend[l, u, 2] = total(1, 48, 48).astype(BF16)
-        ring_copy(l, u, 2).start()
-        rsend[l, u, 3] = total(3, 0, 48).astype(BF16)
-        ring_copy(l, u, 3).start()
-        keep[u, rows(1, 0, 48), :] = total(1, 0, 48)
-        keep[u, rows(3, 48, 48), :] = total(3, 48, 48)
+        if RING[l]:
+            for i, o, lo in ((0, 2, 0), (1, 2, 48), (2, 1, 48), (3, 3, 0)):
+                sends[l][u, i] = total(o, lo, 48).astype(BF16)
+                ring_copy(l, u, i).start()
+            keep[u, rows(1, 0, 48), :] = total(1, 0, 48)
+            keep[u, rows(3, 48, 48), :] = total(3, 48, 48)
+        else:
+            for o in (2, 1, 3):
+                sends[l][u, o - 1] = total(o, 0, ROWS).astype(BF16)
+                ring_copy(l, u, o - 1).start()
         keep[u, rows(0, 0, ROWS), :] = total(0, 0, ROWS)
 
     def stage_c(l, u):
@@ -188,23 +196,28 @@
         up = pl.ds(pl.multiple_of(lax.rem(p + 1, 4) * ROWS, 16), 48)
         down = pl.ds(pl.multiple_of(lax.rem(p + 3, 4) * ROWS + 48, 16), 48)
         ring_copy(l, u, 0).wait_recv()
-        rsend[l, u, 4] = (keep[u, up, :] + rrecv[l, u, 0].astype(F32)).astype(BF16)
+        sends[l][u, 4] = (keep[u, up, :] + recvs[l][u, 0].astype(F32)).astype(BF16)
         ring_copy(l, u, 4).start()
         ring_copy(l, u, 1).wait_recv()
-        rsend[l, u, 5] = (keep[u, down, :] + rrecv[l, u, 1].astype(F32)).astype(BF16)
+        sends[l][u, 5] = (keep[u, down, :] + recvs[l][u, 1].astype(F32)).astype(BF16)
         ring_copy(l, u, 5).start()
 
     def stage_d(l, u):
         t = kind(l, u)
         p = jnp.where(t == 0, x, y)
         q = jnp.where(t == 0, y, x)
-        for i in (2, 3, 4, 5):
+        for i in (2, 3, 4, 5) if RING[l] else (0, 2, 1):
             ring_copy(l, u, i).wait_recv()
+        got = recvs[l]
         r0 = pl.multiple_of(p * ROWS, 16)
-        half0 = keep[u, pl.ds(r0, 48), :] + rrecv[l, u, 3].astype(F32) + rrecv[l, u, 4].astype(F32)
-        half1 = keep[u, pl.ds(r0 + 48, 48), :] + rrecv[l, u, 2].astype(F32) + rrecv[l, u, 5].astype(F32)
-        tbuf[pl.ds(0, 2)] = half0.reshape(2, 24, 256)
-        tbuf[pl.ds(2, 2)] = half1.reshape(2, 24, 256)
+        if RING[l]:
+            half0 = keep[u, pl.ds(r0, 48), :] + got[u, 3].astype(F32) + got[u, 4].astype(F32)
+            half1 = keep[u, pl.ds(r0 + 48, 48), :] + got[u, 2].astype(F32) + got[u, 5].astype(F32)
+            tbuf[pl.ds(0, 2)] = half0.reshape(2, 24, 256)
+            tbuf[pl.ds(2, 2)] = half1.reshape(2, 24, 256)
+        else:
+            whole = keep[u, pl.ds(r0, ROWS), :] + got[u, 0].astype(F32) + got[u, 1].astype(F32) + got[u, 2].astype(F32)
+            tbuf[...] = whole.reshape(4, 24, 256)
         for o in (2, 1, 3):
             v = tbuf[lax.rem(q + o, 4)]
             ysend[l, u, o - 1] = jnp.concatenate([v[:, :128], v[:, 128:]], axis=0).astype(BF16)
@@ -218,27 +231,23 @@
         s = yrecv[l, u, 0].astype(F32) + yrecv[l, u, 1].astype(F32) + yrecv[l, u, 2].astype(F32)
         zb[tap_of(u), :, pl.ds(n0, 256)] = yown[u] + jnp.concatenate([s[:24], s[24:]], axis=1)
 
-    def stage_z(l):
-        v = zb[...].reshape(72, C)
-        pad = jnp.zeros((8, 128), F32)
+    def stage_z(l, g):
+        v = zb[TAPS[g]]
         for zz in range(NZ):
-            part = v[:, zz * 96 : zz * 96 + 96]
-            part = jnp.concatenate([part, jnp.zeros((72, 32), F32)], axis=1)
+            part = jnp.concatenate([v[:, zz * 96 : zz * 96 + 96], jnp.zeros((24, 32), F32)], axis=1)
             zf[zz] = part
-            zs[l, zz] = jnp.concatenate([part, pad], axis=0).astype(BF16)
+            zs[l, g, zz] = jnp.concatenate([part, jnp.zeros((8, 128), F32)], axis=0).astype(BF16)
         for o in (4, 3, 5, 2, 6, 1, 7):
-            z_copy(l, o).start()
-        zown[l] = zf[z]
-
-    def stage_last(l):
+            z_copy(l, g, o).start()
+        zown[l, g] = zf[z]
+
+    def stage_last(l, g):
         for o in (1, 7, 2, 6, 3, 5, 4):
-            z_copy(l, o).wait_recv()
-        tot = zown[l]
+            z_copy(l, g, o).wait_recv()
+        tot = zown[l, g]
         for o in range(1, NZ):
-            tot = tot + zr[l, o - 1].astype(F32)[:72]
-        tot = (tot * SCALE).reshape(3, 24, 128)
-        gw[l] = tot[:, :, :96]
-
+            tot = tot + zr[l, g, o - 1].astype(F32)[:24]
+        gw[l, TAPS[g]] = (tot * SCALE)[:, :96]
 
     def matmul(l, m):
         d = DIL[l]
@@ -281,22 +290,21 @@
         ws = pl.ds(2 * m, 2)
         return pltpu.make_async_copy(stage.at[ws], gin.at[ws], out_sem.at[m])
 
-    bufs = (sa0, sa1, sa2, sa3)
-    places = (c, x, y, z)
-    counts = (2, NX, NY, NZ)
-    first = (0, 1, 4, 7)
+    bufs = (sa0, sa1, sa2)
+    places = (c, y * NX + x, z)
+    counts = (2, NX * NY, NZ)
+    first = (0, 1, NX * NY)
 
     def stat_copy(e, ax, o, sending):
-        n = counts[ax]
-        slot = places[ax] if sending else lax.rem(places[ax] + n - o, n)
         lo, cnt = ((0, 1), (1, 3))[e]
-        to = (
-            dict(to_seq=sid(y, x, 1 - c)),
-            dict(to_seq=sid(y, lax.rem(x + o, NX), c)),
-            dict(to_seq=sid(lax.rem(y + o, NY), x, c)),
-            dict(to_z=lax.rem(z + o, NZ)),
-        )[ax]
-        ref = bufs[ax].at[slot, pl.ds(lo, cnt)]
+        if ax == 0:
+            to, back = dict(to_seq=sid(y, x, 1 - c)), 1 - c
+        elif ax == 1:
+            to = dict(to_seq=plane(o))
+            back = lax.rem(y + NY - o // NX, NY) * NX + lax.rem(x + NX - o % NX, NX)
+        else:
+            to, back = dict(to_z=lax.rem(z + o, NZ)), lax.rem(z + NZ - o, NZ)
+        ref = bufs[ax].at[places[ax] if sending else back, pl.ds(lo, cnt)]
         i = first[ax] + o - 1
         return rdma(ref, ref, st_s.at[e, i], st_r.at[e, i], **to)
 
@@ -318,7 +326,7 @@
         tot = bufs[ax][0, lo : lo + cnt]
         for i in range(1, counts[ax]):
             tot = tot + bufs[ax][i, lo : lo + cnt]
-        if ax < 3:
+        if ax < 2:
             bufs[ax + 1][places[ax + 1], lo : lo + cnt] = tot
         else:
             tot = tot * SCALE
@@ -334,54 +342,27 @@
     def _(w):
         forward(1, w)
 
+    ld_x[0].wait()
+
+    @pl.loop(0, W)
+    def _(w):
+        forward(0, w)
+
     ld_c.wait()
 
-    def grad_weight(l, before):
-        @pl.loop(0, UNITS)
-        def _(u):
-            @pl.when(u == 3)
-            def _():
-                before()
-
-            stage_a(l, u)
-
-            @pl.when(u >= 1)
-            def _():
-                stage_b(l, u - 1)
-
-            @pl.when(u >= 3)
-            def _():
-                stage_c(l, u - 3)
-
-        stage_b(l, UNITS - 1)
-
-    def drain(l, m):
-        @pl.loop(0, 3)
-        def _(i):
-            @pl.when(m == 0)
-            def _():
-                stage_c(l, 6 + i)
-
-            @pl.when(m < 3)
-            def _():
-                stage_d(l, 3 * m + i)
-
-            @pl.when(m >= 1)
-            def _():
-                stage_e(l, 3 * m - 3 + i)
-
-    def halo1_in():
-        for h in halo1():
-            h.wait_recv()
-        clear_ends(1)
-
-    def halo0_in():
-        for m in range(4):
-            for h in halo0(m):
-                h.wait_recv()
-        clear_ends(0)
-
-    grad_weight(1, halo1_in)
+    @pl.loop(0, 3)
+    def _(u):
+        stage_a(1, u)
+
+    for h in halo1():
+        h.wait_recv()
+    clear_ends(1)
+
+    @pl.loop(3, UNITS)
+    def _(u):
+        stage_a(1, u)
+        stage_b(1, u - 3)
+
     ld_w[1].wait()
 
     @pl.loop(0, 4)
@@ -390,21 +371,47 @@
         backward(1, m)
         for h in halo0(m):
             h.start()
-        drain(1, m)
-
-    stage_z(1)
-    ld_x[0].wait()
-
-    @pl.loop(0, W)
-    def _(w):
-        forward(0, w)
+
+        @pl.loop(0, 3)
+        def _(i):
+            @pl.when(m == 0)
+            def _():
+                stage_b(1, 6 + i)
+
+            if RING[1]:
+
+                @pl.when(m < 3)
+                def _():
+                    stage_c(1, 3 * m + i)
+
+            @pl.when(m >= 2)
+            def _():
+                stage_d(1, 3 * (m - 2) + i)
 
     stat_put(1)
     stat_send(1, 0)
-    grad_weight(0, halo0_in)
+
+    @pl.loop(0, 3)
+    def _(u):
+        stage_a(0, u)
+        stage_d(1, 6 + u)
+        stage_e(1, u)
+
     stat_recv(1, 0)
     stat_send(1, 1)
-    stage_last(1)
+    for m in range(4):
+        for h in halo0(m):
+            h.wait_recv()
+    clear_ends(0)
+
+    @pl.loop(3, UNITS)
+    def _(u):
+        stage_a(0, u)
+        stage_b(0, u - 3)
+        stage_e(1, u)
+
+    for g in range(3):
+        stage_z(1, g)
     ld_w[0].wait()
 
     @pl.loop(0, 4)
@@ -412,24 +419,66 @@
         matmul(0, m)
         backward(0, m)
         out_copy(m).start()
-        drain(0, m)
-
+
+        @pl.loop(0, 3)
+        def _(i):
+            @pl.when(m == 0)
+            def _():
+                stage_b(0, 6 + i)
+
+            if RING[0]:
+
+                @pl.when(m < 3)
+                def _():
+                    stage_c(0, 3 * m + i)
+
+                @pl.when(m >= 2)
+                def _():
+                    stage_d(0, 3 * (m - 2) + i)
+
+            else:
+
+                @pl.when(m >= 2)
+                def _():
+                    stage_d(0, 3 * (m - 2) + i)
+
+    stat_put(0)
+    stat_send(0, 0)
     stat_recv(1, 1)
     stat_send(1, 2)
-    stat_put(0)
-    stat_send(0, 0)
-    stage_z(0)
-    stat_recv(1, 2)
-    stat_send(1, 3)
     stat_recv(0, 0)
     stat_send(0, 1)
+    for g in range(3):
+        stage_last(1, g)
+
+    @pl.loop(6, UNITS)
+    def _(u):
+        stage_d(0, u)
+
+    @pl.loop(0, 3)
+    def _(u):
+        stage_e(0, u)
+
+    stage_z(0, 0)
+
+    @pl.loop(3, 6)
+    def _(u):
+        stage_e(0, u)
+
+    stage_z(0, 1)
     stat_recv(0, 1)
     stat_send(0, 2)
+
+    @pl.loop(6, UNITS)
+    def _(u):
+        stage_e(0, u)
+
+    stage_z(0, 2)
+    stat_recv(1, 2)
+    stage_last(0, 0)
+    stage_last(0, 1)
     stat_recv(0, 2)
-    stat_send(0, 3)
-    stage_last(0)
-    stat_recv(1, 3)
-    stat_recv(0, 3)
+    stage_last(0, 2)
 
     for h in halo1():
         h.wait_send()
@@ -445,22 +494,36 @@
         @pl.loop(0, UNITS)
         def _(u, l=l):
             core_copy(l, u).wait_send()
-            for i in range(6):
+            for i in range(6 if RING[l] else 3):
                 ring_copy(l, u, i).wait_send()
             for o in range(1, 4):
                 far_copy(l, u, o).wait_send()
 
-        for o in range(1, NZ):
-            z_copy(l, o).wait_send()
+        for g in range(3):
+            for o in range(1, NZ):
+                z_copy(l, g, o).wait_send()
     for e in range(2):
-        for ax in range(4):
+        for ax in range(3):
             for o in range(1, counts[ax]):
                 stat_copy(e, ax, o, True).wait_send()
+
+
+def last_copy(a, b, c, a_out, b_out, c_out, sem):
+    copies = [pltpu.make_async_copy(a.at[w], a_out.at[w], sem.at[w]) for w in range(W)]
+    copies += [pltpu.make_async_copy(b, b_out, sem.at[W]), pltpu.make_async_copy(c, c_out, sem.at[W + 1])]
+    for copy in copies:
+        copy.start()
+    for copy in copies:
+        copy.wait()
 
 
 def local(saved, cotangent, gain, weight):
     wt = weight.transpose(0, 2, 1, 3)
     dma = pltpu.SemaphoreType.DMA
+
+    def part(l):
+        return (6, 48) if RING[l] else (3, 96)
+
     vm = pltpu.VMEM
     scratch = dict(
         xv=vm((2, W, B, C), BF16),
@@ -476,22 +539,23 @@
         csend=vm((2, UNITS, 384, 256), BF16),
         crecv=vm((2, UNITS, 384, 256), BF16),
         keep=vm((UNITS, 384, 256), F32),
-        rsend=vm((2, UNITS, 6, 48, 256), BF16),
-        rrecv=vm((2, UNITS, 6, 48, 256), BF16),
+        rsend0=vm((UNITS, *part(0), 256), BF16),
+        rrecv0=vm((UNITS, *part(0), 256), BF16),
+        rsend1=vm((UNITS, *part(1), 256), BF16),
+        rrecv1=vm((UNITS, *part(1), 256), BF16),
         tbuf=vm((4, 24, 256), F32),
         ysend=vm((2, UNITS, 3, 48, 128), BF16),
         yrecv=vm((2, UNITS, 3, 48, 128), BF16),
         yown=vm((UNITS, 24, 256), F32),
         zb=vm((3, 24, C), F32),
-        zs=vm((2, NZ, 80, 128), BF16),
-        zf=vm((NZ, 72, 128), F32),
-        zr=vm((2, NZ - 1, 80, 128), BF16),
-        zown=vm((2, 72, 128), F32),
+        zs=vm((2, 3, NZ, 32, 128), BF16),
+        zf=vm((NZ, 24, 128), F32),
+        zr=vm((2, 3, NZ - 1, 32, 128), BF16),
+        zown=vm((2, 3, 24, 128), F32),
         sacc=vm((4, 8, C), F32),
         sa0=vm((2, 4, 8, 128), F32),
-        sa1=vm((NX, 4, 8, 128), F32),
-        sa2=vm((NY, 4, 8, 128), F32),
-        sa3=vm((NZ, 4, 8, 128), F32),
+        sa1=vm((NX * NY, 4, 8, 128), F32),
+        sa2=vm((NZ, 4, 8, 128), F32),
         loc_sem=dma((5,)),
         out_sem=dma((4,)),
         halo_s=dma((10,)),
@@ -502,10 +566,10 @@
         r_r=dma((2, UNITS, 6)),
         y_s=dma((2, UNITS, 3)),
         y_r=dma((2, UNITS, 3)),
-        z_s=dma((2, NZ - 1)),
-        z_r=dma((2, NZ - 1)),
-        st_s=dma((2, 14)),
-        st_r=dma((2, 14)),
+        z_s=dma((2, 3, NZ - 1)),
+        z_r=dma((2, 3, NZ - 1)),
+        st_s=dma((2, 23)),
+        st_r=dma((2, 23)),
     )
     names = list(scratch)
 
@@ -537,6 +601,14 @@
         ),
         cost_estimate=pl.CostEstimate(flops=14_500_000_000, bytes_accessed=13_000_000, transcendentals=1_600_000),
     )(saved, cotangent, gain, wt)
+    gin, gw, gs = pl.pallas_call(
+        last_copy,
+        out_shape=tuple(jax.ShapeDtypeStruct(v.shape, v.dtype) for v in (gin, gw, gs)),
+        in_specs=[pl.BlockSpec(memory_space=pl.ANY)] * 3,
+        out_specs=(pl.BlockSpec(memory_space=pl.ANY),) * 3,
+        scratch_shapes=[dma((W + 2,))],
+        compiler_params=pltpu.CompilerParams(has_side_effects=True),
+    )(gin, gw, gs)
     return gin, gw.transpose(0, 2, 1, 3), gs
 
 

time: 91.7 us -> 122 us (1.33)
  the two profiles are of different devices: /device:TPU:2 before, /device:TPU:1 now
where the time goes in v2:
time: 122 us
  Pallas kernels  122 us (100%)
    pallas_call x1, Pallas kernels, local(): pl.pallas_call(kernel, out_shape=(jax.ShapeDtypeStruct((W, B, C), BF16),...  70.2 us
    pallas_call x1, Pallas kernels, local(): pl.pallas_call(last_copy, out_shape=tuple((jax.ShapeDtypeStruct(v.shape,...  51.4 us

profile of v2, /device:TPU:1, one launch (start us, length us, event | category | flops | bytes accessed | tf_op | source)
XLA Modules:
  0.0 122.3 jit_solution(14091229658177368143)
XLA Ops:
  0.6 70.2 %shard_map.67 = (bf16[8,128,768]{2,1,0:T(8,128)(2,1)}, f32[2,3,24,96]{3,2,1,0:T(8,128)}, f32[2,2,768]{2,1,0:T(2,128)}) custom-call(bf16[2,8,128,768]{3,2,1,0:T(8,128)(2,1)} %refs_0_.1, bf16[8,128,768]{2,1,0:T(8,128)(2,1)} %refs_1_.1, f32[2,768]{1,0:T(2,128)} %refs_2_.1, bf16[2,3,768,768]{3,2,1,0:T(8,128)(2,1)} %bitcast.2), custom_call_target="tpu_custom_call" | custom-call | flops 14499999744 | bytes 13000000 | tf_op jit(solution)/shard_map/pallas_call | solution.py:580
  70.8 51.4 %shard_map.68 = (bf16[8,128,768]{2,1,0:T(8,128)(2,1)}, f32[2,3,24,96]{3,2,1,0:T(8,128)}, f32[2,2,768]{2,1,0:T(2,128)}) custom-call(bf16[8,128,768]{2,1,0:T(8,128)(2,1)} %get-tuple-element.9.a, f32[2,3,24,96]{3,2,1,0:T(8,128)} %get-tuple-element.10.b, f32[2,2,768]{2,1,0:T(2,128)} %get-tuple-element.11.c), custom_call_target="tpu_custom_call" | custom-call | tf_op jit(solution)/shard_map/pallas_call | solution.py:604

commit v3 on v2

--- a/solution.py
+++ b/solution.py
@@ -29,10 +29,10 @@
 
 def body(
     saved, cot, gain, weight, gin, gw, gs,
-    xv, wv, c0, c1, at, gp, rstd, run, gbuf, stage,
+    xv, wv, c0, c1, at0, at1, gp, rstd, run, gbuf, stage,
     csend, crecv, keep, rsend0, rrecv0, rsend1, rrecv1, tbuf, ysend, yrecv, yown, zb, zs, zf, zr, zown,
     sacc, sa0, sa1, sa2,
-    loc_sem, out_sem, halo_s, halo_r, c_s, c_r, r_s, r_r, y_s, y_r, z_s, z_r, st_s, st_r,
+    x1_sem, loc_sem, out_sem, halo_s, halo_r, c_s, c_r, r_s, r_r, y_s, y_r, z_s, z_r, st_s, st_r,
 ):
     seq = lax.axis_index("seq")
     z = lax.axis_index("dp")
@@ -40,6 +40,7 @@
     x = lax.rem(lax.div(seq, 2), NX)
     y = lax.div(seq, 2 * NX)
     cots = (c0, c1)
+    ats = (at0, at1)
 
     def sid(yy, xx, cc):
         return (yy * NX + xx) * 2 + cc
@@ -53,14 +54,13 @@
     right = lax.rem(seq + 1, 32)
     left = lax.rem(seq + 31, 32)
 
-    ld_x = [pltpu.make_async_copy(saved.at[l], xv.at[l], loc_sem.at[l]) for l in range(2)]
+    ld_x1 = [pltpu.make_async_copy(saved.at[1, w], xv.at[1, w], x1_sem.at[w]) for w in range(W)]
+    ld_x0 = pltpu.make_async_copy(saved.at[0], xv.at[0], loc_sem.at[0])
     ld_c = pltpu.make_async_copy(cot, c1.at[:, pl.ds(DIL[1], B), :], loc_sem.at[2])
     ld_w = [pltpu.make_async_copy(weight.at[l], wv.at[l], loc_sem.at[3 + l]) for l in range(2)]
-    ld_x[1].start()
+    for ld in ld_x1:
+        ld.start()
     ld_c.start()
-    ld_w[1].start()
-    ld_x[0].start()
-    ld_w[0].start()
 
     def plane(o):
         return sid(lax.rem(y + o // NX, NY), lax.rem(x + o % NX, NX), c)
@@ -124,7 +124,7 @@
                         yy, xx = (other, dest) if t_ == 0 else (dest, other)
                         r0 = sid(yy, xx, cc) * 24
                         parts.append(a[r0 : r0 + 24])
-                at[l, t_, cc, :, cols] = jnp.concatenate(parts, axis=0).astype(BF16)
+                ats[l][t_, cc, :, cols] = jnp.concatenate(parts, axis=0).astype(BF16)
 
     def kind(l, u):
         return lax.rem(u + (1 - l), 2)
@@ -156,15 +156,17 @@
         to = lax.rem(z + o, NZ)
         return rdma(zs.at[l, g, to], zr.at[l, g, o - 1], z_s.at[l, g, o - 1], z_r.at[l, g, o - 1], to_z=to)
 
-    def stage_a(l, u):
+    def stage_a(l, u, beside=None):
         d = DIL[l]
         t = kind(l, u)
         off = pl.multiple_of(lax.rem(lax.div(u, 3) + 1, 3) * d, 16)
         n0 = pl.multiple_of(lax.rem(u, 3) * 256, 256)
         rhs = cots[l][:, pl.ds(off, B), pl.ds(n0, 256)].reshape(W * B, 256)
-        csend[l, u] = jnp.dot(at[l, t, 1 - c], rhs, preferred_element_type=F32).astype(BF16)
+        csend[l, u] = jnp.dot(ats[l][t, 1 - c], rhs, preferred_element_type=F32).astype(BF16)
+        keep[l, u] = jnp.dot(ats[l][t, c], rhs, preferred_element_type=F32)
+        if beside is not None:
+            beside()
         core_copy(l, u).start()
-        keep[u] = jnp.dot(at[l, t, c], rhs, preferred_element_type=F32)
 
     def stage_b(l, u):
         t = kind(l, u)
@@ -176,19 +178,19 @@
 
         def total(o, lo, n):
             r = rows(o, lo, n)
-            return keep[u, r, :] + crecv[l, u, r, :].astype(F32)
+            return keep[l, u, r, :] + crecv[l, u, r, :].astype(F32)
 
         if RING[l]:
             for i, o, lo in ((0, 2, 0), (1, 2, 48), (2, 1, 48), (3, 3, 0)):
                 sends[l][u, i] = total(o, lo, 48).astype(BF16)
                 ring_copy(l, u, i).start()
-            keep[u, rows(1, 0, 48), :] = total(1, 0, 48)
-            keep[u, rows(3, 48, 48), :] = total(3, 48, 48)
+            keep[l, u, rows(1, 0, 48), :] = total(1, 0, 48)
+            keep[l, u, rows(3, 48, 48), :] = total(3, 48, 48)
         else:
             for o in (2, 1, 3):
                 sends[l][u, o - 1] = total(o, 0, ROWS).astype(BF16)
                 ring_copy(l, u, o - 1).start()
-        keep[u, rows(0, 0, ROWS), :] = total(0, 0, ROWS)
+        keep[l, u, rows(0, 0, ROWS), :] = total(0, 0, ROWS)
 
     def stage_c(l, u):
         t = kind(l, u)
@@ -196,10 +198,10 @@
         up = pl.ds(pl.multiple_of(lax.rem(p + 1, 4) * ROWS, 16), 48)
         down = pl.ds(pl.multiple_of(lax.rem(p + 3, 4) * ROWS + 48, 16), 48)
         ring_copy(l, u, 0).wait_recv()
-        sends[l][u, 4] = (keep[u, up, :] + recvs[l][u, 0].astype(F32)).astype(BF16)
+        sends[l][u, 4] = (keep[l, u, up, :] + recvs[l][u, 0].astype(F32)).astype(BF16)
         ring_copy(l, u, 4).start()
         ring_copy(l, u, 1).wait_recv()
-        sends[l][u, 5] = (keep[u, down, :] + recvs[l][u, 1].astype(F32)).astype(BF16)
+        sends[l][u, 5] = (keep[l, u, down, :] + recvs[l][u, 1].astype(F32)).astype(BF16)
         ring_copy(l, u, 5).start()
 
     def stage_d(l, u):
@@ -211,12 +213,12 @@
         got = recvs[l]
         r0 = pl.multiple_of(p * ROWS, 16)
         if RING[l]:
-            half0 = keep[u, pl.ds(r0, 48), :] + got[u, 3].astype(F32) + got[u, 4].astype(F32)
-            half1 = keep[u, pl.ds(r0 + 48, 48), :] + got[u, 2].astype(F32) + got[u, 5].astype(F32)
+            half0 = keep[l, u, pl.ds(r0, 48), :] + got[u, 3].astype(F32) + got[u, 4].astype(F32)
+            half1 = keep[l, u, pl.ds(r0 + 48, 48), :] + got[u, 2].astype(F32) + got[u, 5].astype(F32)
             tbuf[pl.ds(0, 2)] = half0.reshape(2, 24, 256)
             tbuf[pl.ds(2, 2)] = half1.reshape(2, 24, 256)
         else:
-            whole = keep[u, pl.ds(r0, ROWS), :] + got[u, 0].astype(F32) + got[u, 1].astype(F32) + got[u, 2].astype(F32)
+            whole = keep[l, u, pl.ds(r0, ROWS), :] + got[u, 0].astype(F32) + got[u, 1].astype(F32) + got[u, 2].astype(F32)
             tbuf[...] = whole.reshape(4, 24, 256)
         for o in (2, 1, 3):
             v = tbuf[lax.rem(q + o, 4)]
@@ -336,33 +338,33 @@
                     gs[a, b : b + 1, j * 128 : j * 128 + 128] = tot[i, j : j + 1, :]
 
     sacc[...] = jnp.zeros_like(sacc)
-    ld_x[1].wait()
+    ld_x0.start()
 
     @pl.loop(0, W)
     def _(w):
+        pltpu.make_async_copy(saved.at[1, w], xv.at[1, w], x1_sem.at[w]).wait()
         forward(1, w)
 
-    ld_x[0].wait()
-
-    @pl.loop(0, W)
-    def _(w):
-        forward(0, w)
-
+    ld_w[1].start()
+    ld_w[0].start()
     ld_c.wait()
+    ld_x0.wait()
 
     @pl.loop(0, 3)
     def _(u):
-        stage_a(1, u)
+        stage_a(1, u, lambda: forward(0, u))
 
     for h in halo1():
         h.wait_recv()
     clear_ends(1)
 
-    @pl.loop(3, UNITS)
+    @pl.loop(3, 8)
     def _(u):
-        stage_a(1, u)
+        stage_a(1, u, lambda: forward(0, u))
         stage_b(1, u - 3)
 
+    stage_a(1, 8)
+    stage_b(1, 5)
     ld_w[1].wait()
 
     @pl.loop(0, 4)
@@ -380,13 +382,9 @@
 
             if RING[1]:
 
-                @pl.when(m < 3)
+                @pl.when(m >= 1)
                 def _():
-                    stage_c(1, 3 * m + i)
-
-            @pl.when(m >= 2)
-            def _():
-                stage_d(1, 3 * (m - 2) + i)
+                    stage_c(1, 3 * m - 3 + i)
 
     stat_put(1)
     stat_send(1, 0)
@@ -394,8 +392,7 @@
     @pl.loop(0, 3)
     def _(u):
         stage_a(0, u)
-        stage_d(1, 6 + u)
-        stage_e(1, u)
+        stage_d(1, u)
 
     stat_recv(1, 0)
     stat_send(1, 1)
@@ -408,10 +405,8 @@
     def _(u):
         stage_a(0, u)
         stage_b(0, u - 3)
-        stage_e(1, u)
-
-    for g in range(3):
-        stage_z(1, g)
+        stage_d(1, u)
+
     ld_w[0].wait()
 
     @pl.loop(0, 4)
@@ -432,15 +427,13 @@
                 def _():
                     stage_c(0, 3 * m + i)
 
-                @pl.when(m >= 2)
-                def _():
-                    stage_d(0, 3 * (m - 2) + i)
-
-            else:
-
-                @pl.when(m >= 2)
-                def _():
-                    stage_d(0, 3 * (m - 2) + i)
+            @pl.when(m == 3)
+            def _():
+                stage_d(0, i)
+
+            @pl.when(m >= 1)
+            def _():
+                stage_e(1, 3 * m - 3 + i)
 
     stat_put(0)
     stat_send(0, 0)
@@ -449,36 +442,29 @@
     stat_recv(0, 0)
     stat_send(0, 1)
     for g in range(3):
-        stage_last(1, g)
-
-    @pl.loop(6, UNITS)
+        stage_z(1, g)
+
+    @pl.loop(3, UNITS)
     def _(u):
         stage_d(0, u)
 
-    @pl.loop(0, 3)
-    def _(u):
-        stage_e(0, u)
-
-    stage_z(0, 0)
-
-    @pl.loop(3, 6)
-    def _(u):
-        stage_e(0, u)
-
-    stage_z(0, 1)
     stat_recv(0, 1)
     stat_send(0, 2)
-
-    @pl.loop(6, UNITS)
-    def _(u):
-        stage_e(0, u)
-
-    stage_z(0, 2)
-    stat_recv(1, 2)
-    stage_last(0, 0)
-    stage_last(0, 1)
+    for g in range(3):
+
+        @pl.loop(3 * g, 3 * g + 3)
+        def _(u):
+            stage_e(0, u)
+
+        stage_z(0, g)
+        if g == 0:
+            for k in range(3):
+                stage_last(1, k)
+            stat_recv(1, 2)
+
     stat_recv(0, 2)
-    stage_last(0, 2)
+    for g in range(3):
+        stage_last(0, g)
 
     for h in halo1():
         h.wait_send()
@@ -508,12 +494,17 @@
                 stat_copy(e, ax, o, True).wait_send()
 
 
-def last_copy(a, b, c, a_out, b_out, c_out, sem):
-    copies = [pltpu.make_async_copy(a.at[w], a_out.at[w], sem.at[w]) for w in range(W)]
-    copies += [pltpu.make_async_copy(b, b_out, sem.at[W]), pltpu.make_async_copy(c, c_out, sem.at[W + 1])]
-    for copy in copies:
+def last_copy(a, b, c, a_out, b_out, c_out, at, sem):
+    into = [pltpu.make_async_copy(a.at[w], at.at[w], sem.at[w]) for w in range(W)]
+    out = [pltpu.make_async_copy(at.at[w], a_out.at[w], sem.at[W + w]) for w in range(W)]
+    for copy in into:
         copy.start()
-    for copy in copies:
+    b_out[...] = b[...]
+    c_out[...] = c[...]
+    for first, second in zip(into, out):
+        first.wait()
+        second.start()
+    for copy in out:
         copy.wait()
 
 
@@ -530,7 +521,8 @@
         wv=vm((2, 3, C, C), BF16),
         c0=vm((W, B + 2 * DIL[0], C), BF16),
         c1=vm((W, B + 2 * DIL[1], C), BF16),
-        at=vm((2, 2, 2, 384, W * B), BF16),
+        at0=vm((2, 2, 384, W * B), BF16),
+        at1=vm((2, 2, 384, W * B), BF16),
         gp=vm((2, W, B, C), F32),
         rstd=vm((2, W, B, 128), F32),
         run=vm((W, B, C), F32),
@@ -538,7 +530,7 @@
         stage=vm((W, B, C), BF16),
         csend=vm((2, UNITS, 384, 256), BF16),
         crecv=vm((2, UNITS, 384, 256), BF16),
-        keep=vm((UNITS, 384, 256), F32),
+        keep=vm((2, UNITS, 384, 256), F32),
         rsend0=vm((UNITS, *part(0), 256), BF16),
         rrecv0=vm((UNITS, *part(0), 256), BF16),
         rsend1=vm((UNITS, *part(1), 256), BF16),
@@ -556,6 +548,7 @@
         sa0=vm((2, 4, 8, 128), F32),
         sa1=vm((NX * NY, 4, 8, 128), F32),
         sa2=vm((NZ, 4, 8, 128), F32),
+        x1_sem=dma((W,)),
         loc_sem=dma((5,)),
         out_sem=dma((4,)),
         halo_s=dma((10,)),
@@ -604,9 +597,9 @@
     gin, gw, gs = pl.pallas_call(
         last_copy,
         out_shape=tuple(jax.ShapeDtypeStruct(v.shape, v.dtype) for v in (gin, gw, gs)),
-        in_specs=[pl.BlockSpec(memory_space=pl.ANY)] * 3,
-        out_specs=(pl.BlockSpec(memory_space=pl.ANY),) * 3,
-        scratch_shapes=[dma((W + 2,))],
+        in_specs=[pl.BlockSpec(memory_space=pl.ANY)] + [pl.BlockSpec(memory_space=vm)] * 2,
+        out_specs=(pl.BlockSpec(memory_space=pl.ANY),) + (pl.BlockSpec(memory_space=vm),) * 2,
+        scratch_shapes=[vm((W, B, C), BF16), dma((2 * W,))],
         compiler_params=pltpu.CompilerParams(has_side_effects=True),
     )(gin, gw, gs)
     return gin, gw.transpose(0, 2, 1, 3), gs

time: 122 us -> 70.7 us (0.58)
  Pallas kernels: 122 us -> 69.5 us
    pallas_call x1, Pallas kernels: 51.4 us -> 3.81 us  [local(): pl.pallas_call(last_copy, out_shape=tuple((jax.ShapeDtypeStruct(v.shape,...]
    pallas_call x1, Pallas kernels: 70.2 us -> 65.7 us  [local(): pl.pallas_call(kernel, out_shape=(jax.ShapeDtypeStruct((W, B, C), BF16),...]
where the time goes in v3:
time: 70.7 us; the launch traced here: 70.1 us
  Pallas kernels  69.5 us (98%)
    pallas_call x1, Pallas kernels, local(): pl.pallas_call(kernel, out_shape=(jax.ShapeDtypeStruct((W, B, C), BF16),...  65.7 us
    pallas_call x1, Pallas kernels, local(): pl.pallas_call(last_copy, out_shape=tuple((jax.ShapeDtypeStruct(v.shape,...  3.81 us

profile of v3, /device:TPU:1, one launch (start us, length us, event | category | flops | bytes accessed | tf_op | source)
XLA Modules:
  0.0 70.1 jit_solution(1294312660585593108)
XLA Ops:
  0.6 65.7 %shard_map.67 = (bf16[8,128,768]{2,1,0:T(8,128)(2,1)}, f32[2,3,24,96]{3,2,1,0:T(8,128)}, f32[2,2,768]{2,1,0:T(2,128)}) custom-call(bf16[2,8,128,768]{3,2,1,0:T(8,128)(2,1)} %refs_0_.1, bf16[8,128,768]{2,1,0:T(8,128)(2,1)} %refs_1_.1, f32[2,768]{1,0:T(2,128)} %refs_2_.1, bf16[2,3,768,768]{3,2,1,0:T(8,128)(2,1)} %bitcast.2), custom_call_target="tpu_custom_call" | custom-call | flops 14499999744 | bytes 13000000 | tf_op jit(solution)/shard_map/pallas_call | solution.py:573
  66.3 3.8 %shard_map.68 = (bf16[8,128,768]{2,1,0:T(8,128)(2,1)}, f32[2,3,24,96]{3,2,1,0:T(8,128)}, f32[2,2,768]{2,1,0:T(2,128)}) custom-call(bf16[8,128,768]{2,1,0:T(8,128)(2,1)} %get-tuple-element.9.a, f32[2,3,24,96]{3,2,1,0:T(8,128)} %get-tuple-element.10.b, f32[2,2,768]{2,1,0:T(2,128)} %get-tuple-element.11.c), custom_call_target="tpu_custom_call" | custom-call | tf_op jit(solution)/shard_map/pallas_call | solution.py:597

commit v4 on v3

--- a/solution.py
+++ b/solution.py
@@ -21,7 +21,6 @@
 UNITS = 9
 ROWS = 96
 TAPS = (1, 0, 2)
-RING = (False, True)
 K0 = math.sqrt(2.0 / math.pi)
 K1 = 0.044715
 SCALE = 1.0 / math.sqrt(64 * 4096)
@@ -29,10 +28,10 @@
 
 def body(
     saved, cot, gain, weight, gin, gw, gs,
-    xv, wv, c0, c1, at0, at1, gp, rstd, run, gbuf, stage,
-    csend, crecv, keep, rsend0, rrecv0, rsend1, rrecv1, tbuf, ysend, yrecv, yown, zb, zs, zf, zr, zown,
+    xv, wv, c0, c1, at0, at1, gp, rstd, run, gbuf,
+    csend, crecv, keep, rsend, rrecv, tbuf, ysend, yrecv, yown, zb, zs, zf, zr, zown,
     sacc, sa0, sa1, sa2,
-    x1_sem, loc_sem, out_sem, halo_s, halo_r, c_s, c_r, r_s, r_r, y_s, y_r, z_s, z_r, st_s, st_r,
+    x1_sem, loc_sem, halo_s, halo_r, c_s, c_r, r_s, r_r, y_s, y_r, z_s, z_r, st_s, st_r,
 ):
     seq = lax.axis_index("seq")
     z = lax.axis_index("dp")
@@ -129,31 +128,33 @@
     def kind(l, u):
         return lax.rem(u + (1 - l), 2)
 
+    along_x = [seq] + [sid(y, lax.rem(x + o, NX), c) for o in range(1, NX)]
+    along_y = [seq] + [sid(lax.rem(y + o, NY), x, c) for o in range(1, NY)]
+    along_z = [lax.rem(z + o, NZ) for o in range(NZ)]
+    twin = seq + 1 - 2 * c
+
     def near(t, o):
-        return jnp.where(t == 0, sid(y, lax.rem(x + o, NX), c), sid(lax.rem(y + o, NY), x, c))
+        return jnp.where(t == 0, along_x[o], along_y[o])
 
     def far(t, o):
-        return jnp.where(t == 0, sid(lax.rem(y + o, NY), x, c), sid(y, lax.rem(x + o, NX), c))
+        return jnp.where(t == 0, along_y[o], along_x[o])
 
     def tap_of(u):
         return 2 - lax.rem(lax.div(u, 3) + 1, 3)
 
     def core_copy(l, u):
-        return rdma(csend.at[l, u], crecv.at[l, u], c_s.at[l, u], c_r.at[l, u], to_seq=sid(y, x, 1 - c))
-
-    sends, recvs = (rsend0, rsend1), (rrecv0, rrecv1)
-
-    def ring_copy(l, u, i):
-        o = (1 if i in (0, 2, 4) else 3) if RING[l] else i + 1
+        return rdma(csend.at[l, u], crecv.at[l, u], c_s.at[l, u], c_r.at[l, u], to_seq=twin)
+
+    def ring_copy(l, u, o):
         return rdma(
-            sends[l].at[u, i], recvs[l].at[u, i], r_s.at[l, u, i], r_r.at[l, u, i], to_seq=near(kind(l, u), o)
+            rsend.at[l, u, o - 1], rrecv.at[l, u, o - 1], r_s.at[l, u, o - 1], r_r.at[l, u, o - 1], to_seq=near(kind(l, u), o)
         )
 
     def far_copy(l, u, o):
         return rdma(ysend.at[l, u, o - 1], yrecv.at[l, u, o - 1], y_s.at[l, u, o - 1], y_r.at[l, u, o - 1], to_seq=far(kind(l, u), o))
 
     def z_copy(l, g, o):
-        to = lax.rem(z + o, NZ)
+        to = along_z[o]
         return rdma(zs.at[l, g, to], zr.at[l, g, o - 1], z_s.at[l, g, o - 1], z_r.at[l, g, o - 1], to_z=to)
 
     def stage_a(l, u, beside=None):
@@ -173,53 +174,28 @@
         p = jnp.where(t == 0, x, y)
         core_copy(l, u).wait_recv()
 
-        def rows(o, lo, n):
-            return pl.ds(pl.multiple_of(lax.rem(p + o, 4) * ROWS + lo, 16), n)
-
-        def total(o, lo, n):
-            r = rows(o, lo, n)
+        def rows(o):
+            return pl.ds(pl.multiple_of(lax.rem(p + o, 4) * ROWS, 16), ROWS)
+
+        def total(o):
+            r = rows(o)
             return keep[l, u, r, :] + crecv[l, u, r, :].astype(F32)
 
-        if RING[l]:
-            for i, o, lo in ((0, 2, 0), (1, 2, 48), (2, 1, 48), (3, 3, 0)):
-                sends[l][u, i] = total(o, lo, 48).astype(BF16)
-                ring_copy(l, u, i).start()
-            keep[l, u, rows(1, 0, 48), :] = total(1, 0, 48)
-            keep[l, u, rows(3, 48, 48), :] = total(3, 48, 48)
-        else:
-            for o in (2, 1, 3):
-                sends[l][u, o - 1] = total(o, 0, ROWS).astype(BF16)
-                ring_copy(l, u, o - 1).start()
-        keep[l, u, rows(0, 0, ROWS), :] = total(0, 0, ROWS)
-
-    def stage_c(l, u):
-        t = kind(l, u)
-        p = jnp.where(t == 0, x, y)
-        up = pl.ds(pl.multiple_of(lax.rem(p + 1, 4) * ROWS, 16), 48)
-        down = pl.ds(pl.multiple_of(lax.rem(p + 3, 4) * ROWS + 48, 16), 48)
-        ring_copy(l, u, 0).wait_recv()
-        sends[l][u, 4] = (keep[l, u, up, :] + recvs[l][u, 0].astype(F32)).astype(BF16)
-        ring_copy(l, u, 4).start()
-        ring_copy(l, u, 1).wait_recv()
-        sends[l][u, 5] = (keep[l, u, down, :] + recvs[l][u, 1].astype(F32)).astype(BF16)
-        ring_copy(l, u, 5).start()
+        for o in (2, 1, 3):
+            rsend[l, u, o - 1] = total(o).astype(BF16)
+            ring_copy(l, u, o).start()
+        keep[l, u, rows(0), :] = total(0)
 
     def stage_d(l, u):
         t = kind(l, u)
         p = jnp.where(t == 0, x, y)
         q = jnp.where(t == 0, y, x)
-        for i in (2, 3, 4, 5) if RING[l] else (0, 2, 1):
-            ring_copy(l, u, i).wait_recv()
-        got = recvs[l]
-        r0 = pl.multiple_of(p * ROWS, 16)
-        if RING[l]:
-            half0 = keep[l, u, pl.ds(r0, 48), :] + got[u, 3].astype(F32) + got[u, 4].astype(F32)
-            half1 = keep[l, u, pl.ds(r0 + 48, 48), :] + got[u, 2].astype(F32) + got[u, 5].astype(F32)
-            tbuf[pl.ds(0, 2)] = half0.reshape(2, 24, 256)
-            tbuf[pl.ds(2, 2)] = half1.reshape(2, 24, 256)
-        else:
-            whole = keep[l, u, pl.ds(r0, ROWS), :] + got[u, 0].astype(F32) + got[u, 1].astype(F32) + got[u, 2].astype(F32)
-            tbuf[...] = whole.reshape(4, 24, 256)
+        for o in (1, 3, 2):
+            ring_copy(l, u, o).wait_recv()
+        whole = keep[l, u, pl.ds(pl.multiple_of(p * ROWS, 16), ROWS), :]
+        for i in range(3):
+            whole = whole + rrecv[l, u, i].astype(F32)
+        tbuf[...] = whole.reshape(4, 24, 256)
         for o in (2, 1, 3):
             v = tbuf[lax.rem(q + o, 4)]
             ysend[l, u, o - 1] = jnp.concatenate([v[:, :128], v[:, 128:]], axis=0).astype(BF16)
@@ -286,11 +262,7 @@
                     c0[w, pl.ds(DIL[0] + q * 64, 64), :] = nb
                     sacc[2] += nb.astype(F32).reshape(8, 8, C).sum(axis=0)
                 else:
-                    stage[w, r, :] = (run[w, r, :] + dx).astype(BF16)
-
-    def out_copy(m):
-        ws = pl.ds(2 * m, 2)
-        return pltpu.make_async_copy(stage.at[ws], gin.at[ws], out_sem.at[m])
+                    gin[w, r, :] = (run[w, r, :] + dx).astype(BF16)
 
     bufs = (sa0, sa1, sa2)
     places = (c, y * NX + x, z)
@@ -358,13 +330,11 @@
         h.wait_recv()
     clear_ends(1)
 
-    @pl.loop(3, 8)
+    @pl.loop(3, 6)
     def _(u):
         stage_a(1, u, lambda: forward(0, u))
         stage_b(1, u - 3)
 
-    stage_a(1, 8)
-    stage_b(1, 5)
     ld_w[1].wait()
 
     @pl.loop(0, 4)
@@ -378,21 +348,27 @@
         def _(i):
             @pl.when(m == 0)
             def _():
-                stage_b(1, 6 + i)
-
-            if RING[1]:
-
-                @pl.when(m >= 1)
-                def _():
-                    stage_c(1, 3 * m - 3 + i)
+                stage_b(1, 3 + i)
+
+            @pl.when(m == 3)
+            def _():
+                stage_d(1, i)
 
     stat_put(1)
     stat_send(1, 0)
+
+    @pl.loop(6, 8)
+    def _(u):
+        stage_a(1, u, lambda: forward(0, u))
+        stage_d(1, u - 3)
+
+    stage_a(1, 8)
+    stage_d(1, 5)
 
     @pl.loop(0, 3)
     def _(u):
         stage_a(0, u)
-        stage_d(1, u)
+        stage_b(1, 6 + u)
 
     stat_recv(1, 0)
     stat_send(1, 1)
@@ -405,15 +381,16 @@
     def _(u):
         stage_a(0, u)
         stage_b(0, u - 3)
-        stage_d(1, u)
-
+        stage_e(1, u - 3)
+
+    stage_z(1, 0)
+    stage_z(1, 1)
     ld_w[0].wait()
 
     @pl.loop(0, 4)
     def _(m):
         matmul(0, m)
         backward(0, m)
-        out_copy(m).start()
 
         @pl.loop(0, 3)
         def _(i):
@@ -421,19 +398,17 @@
             def _():
                 stage_b(0, 6 + i)
 
-            if RING[0]:
-
-                @pl.when(m < 3)
-                def _():
-                    stage_c(0, 3 * m + i)
+            @pl.when(m == 1)
+            def _():
+                stage_d(1, 6 + i)
+
+            @pl.when(m == 2)
+            def _():
+                stage_d(0, i)
 
             @pl.when(m == 3)
             def _():
-                stage_d(0, i)
-
-            @pl.when(m >= 1)
-            def _():
-                stage_e(1, 3 * m - 3 + i)
+                stage_e(1, 6 + i)
 
     stat_put(0)
     stat_send(0, 0)
@@ -441,8 +416,7 @@
     stat_send(1, 2)
     stat_recv(0, 0)
     stat_send(0, 1)
-    for g in range(3):
-        stage_z(1, g)
+    stage_z(1, 2)
 
     @pl.loop(3, UNITS)
     def _(u):
@@ -471,7 +445,6 @@
 
     @pl.loop(0, 4)
     def _(m):
-        out_copy(m).wait()
         for h in halo0(m):
             h.wait_send()
 
@@ -480,8 +453,8 @@
         @pl.loop(0, UNITS)
         def _(u, l=l):
             core_copy(l, u).wait_send()
-            for i in range(6 if RING[l] else 3):
-                ring_copy(l, u, i).wait_send()
+            for o in range(1, 4):
+                ring_copy(l, u, o).wait_send()
             for o in range(1, 4):
                 far_copy(l, u, o).wait_send()
 
@@ -494,26 +467,9 @@
                 stat_copy(e, ax, o, True).wait_send()
 
 
-def last_copy(a, b, c, a_out, b_out, c_out, at, sem):
-    into = [pltpu.make_async_copy(a.at[w], at.at[w], sem.at[w]) for w in range(W)]
-    out = [pltpu.make_async_copy(at.at[w], a_out.at[w], sem.at[W + w]) for w in range(W)]
-    for copy in into:
-        copy.start()
-    b_out[...] = b[...]
-    c_out[...] = c[...]
-    for first, second in zip(into, out):
-        first.wait()
-        second.start()
-    for copy in out:
-        copy.wait()
-
-
 def local(saved, cotangent, gain, weight):
     wt = weight.transpose(0, 2, 1, 3)
     dma = pltpu.SemaphoreType.DMA
-
-    def part(l):
-        return (6, 48) if RING[l] else (3, 96)
 
     vm = pltpu.VMEM
     scratch = dict(
@@ -527,14 +483,11 @@
         rstd=vm((2, W, B, 128), F32),
         run=vm((W, B, C), F32),
         gbuf=vm((2 * B, C), F32),
-        stage=vm((W, B, C), BF16),
         csend=vm((2, UNITS, 384, 256), BF16),
         crecv=vm((2, UNITS, 384, 256), BF16),
         keep=vm((2, UNITS, 384, 256), F32),
-        rsend0=vm((UNITS, *part(0), 256), BF16),
-        rrecv0=vm((UNITS, *part(0), 256), BF16),
-        rsend1=vm((UNITS, *part(1), 256), BF16),
-        rrecv1=vm((UNITS, *part(1), 256), BF16),
+        rsend=vm((2, UNITS, 3, ROWS, 256), BF16),
+        rrecv=vm((2, UNITS, 3, ROWS, 256), BF16),
         tbuf=vm((4, 24, 256), F32),
         ysend=vm((2, UNITS, 3, 48, 128), BF16),
         yrecv=vm((2, UNITS, 3, 48, 128), BF16),
@@ -550,13 +503,12 @@
         sa2=vm((NZ, 4, 8, 128), F32),
         x1_sem=dma((W,)),
         loc_sem=dma((5,)),
-        out_sem=dma((4,)),
         halo_s=dma((10,)),
         halo_r=dma((10,)),
         c_s=dma((2, UNITS)),
         c_r=dma((2, UNITS)),
-        r_s=dma((2, UNITS, 6)),
-        r_r=dma((2, UNITS, 6)),
+        r_s=dma((2, UNITS, 3)),
+        r_r=dma((2, UNITS, 3)),
         y_s=dma((2, UNITS, 3)),
         y_r=dma((2, UNITS, 3)),
         z_s=dma((2, 3, NZ - 1)),
@@ -573,9 +525,9 @@
     gin, gw, gs = pl.pallas_call(
         kernel,
         out_shape=(
-            jax.ShapeDtypeStruct((W, B, C), BF16),
-            jax.ShapeDtypeStruct((2, 3, 24, 96), F32),
-            jax.ShapeDtypeStruct((2, 2, C), F32),
+            vm((W, B, C), BF16),
+            vm((2, 3, 24, 96), F32),
+            vm((2, 2, C), F32),
         ),
         in_specs=[
             pl.BlockSpec(memory_space=pl.ANY),
@@ -584,24 +536,16 @@
             pl.BlockSpec(memory_space=pl.ANY),
         ],
         out_specs=(
-            pl.BlockSpec(memory_space=pl.ANY),
+            pl.BlockSpec(memory_space=pltpu.VMEM),
             pl.BlockSpec(memory_space=pltpu.VMEM),
             pl.BlockSpec(memory_space=pltpu.VMEM),
         ),
         scratch_shapes=list(scratch.values()),
         compiler_params=pltpu.CompilerParams(
-            collective_id=0, has_side_effects=True, vmem_limit_bytes=62 * 1024 * 1024
+            collective_id=0, has_side_effects=True, vmem_limit_bytes=56 * 1024 * 1024
         ),
         cost_estimate=pl.CostEstimate(flops=14_500_000_000, bytes_accessed=13_000_000, transcendentals=1_600_000),
     )(saved, cotangent, gain, wt)
-    gin, gw, gs = pl.pallas_call(
-        last_copy,
-        out_shape=tuple(jax.ShapeDtypeStruct(v.shape, v.dtype) for v in (gin, gw, gs)),
-        in_specs=[pl.BlockSpec(memory_space=pl.ANY)] + [pl.BlockSpec(memory_space=vm)] * 2,
-        out_specs=(pl.BlockSpec(memory_space=pl.ANY),) + (pl.BlockSpec(memory_space=vm),) * 2,
-        scratch_shapes=[vm((W, B, C), BF16), dma((2 * W,))],
-        compiler_params=pltpu.CompilerParams(has_side_effects=True),
-    )(gin, gw, gs)
     return gin, gw.transpose(0, 2, 1, 3), gs
 
 

time: 70.7 us -> 69.5 us (0.983)
  Pallas kernels: 69.5 us -> 66.3 us
  local copies, waits for them, and re-layouts: 0 us -> 2.38 us
    pallas_call x2 -> x1, Pallas kernels: 69.5 us -> 66.3 us  [local(): pl.pallas_call(kernel, out_shape=(vm((W, B, C), BF16), vm((2, 3, 24, 96),...]
    unnamed x0 -> x3, local copies, waits for them, and re-layouts: none -> 2.38 us
where the time goes in v4:
time: 69.5 us; the launch traced here: 69.4 us
  Pallas kernels  66.3 us (95%)
  local copies, waits for them, and re-layouts  2.38 us (3%)
    pallas_call x1, Pallas kernels, local(): pl.pallas_call(kernel, out_shape=(vm((W, B, C), BF16), vm((2, 3, 24, 96),...  66.3 us
    unnamed x3, local copies, waits for them, and re-layouts  2.38 us

profile of v4, /device:TPU:1, one launch (start us, length us, event | category | flops | bytes accessed | tf_op | source)
XLA Modules:
  0.0 69.4 jit_solution(5494801439992032411)
XLA Ops:
  0.6 66.3 %shard_map.67 = (bf16[8,128,768]{2,1,0:T(8,128)(2,1)S(1)}, f32[2,3,24,96]{3,2,1,0:T(8,128)S(1)}, f32[2,2,768]{2,1,0:T(2,128)S(1)}) custom-call(bf16[2,8,128,768]{3,2,1,0:T(8,128)(2,1)} %refs_0_.1, bf16[8,128,768]{2,1,0:T(8,128)(2,1)} %refs_1_.1, f32[2,768]{1,0:T(2,128)} %refs_2_.1, bf16[2,3,768,768]{3,2,1,0:T(8,128)(2,1)} %bitcast.3), custom_call_target="tpu_custom_call" | custom-call | flops 14499999744 | bytes 13000000 | tf_op jit(solution)/shard_map/pallas_call | solution.py:525
  67.0 1.1 %copy.10 = bf16[8,128,768]{2,1,0:T(8,128)(2,1)} copy(bf16[8,128,768]{2,1,0:T(8,128)(2,1)S(1)} %get-tuple-element.9) | data formatting | bytes 3145728
  68.1 0.6 copy.11
  68.8 0.6 copy.12

commit v5 on v4

--- a/solution.py
+++ b/solution.py
@@ -30,7 +30,7 @@
     saved, cot, gain, weight, gin, gw, gs,
     xv, wv, c0, c1, at0, at1, gp, rstd, run, gbuf,
     csend, crecv, keep, rsend, rrecv, tbuf, ysend, yrecv, yown, zb, zs, zf, zr, zown,
-    sacc, sa0, sa1, sa2,
+    sacc, sa0, sa1,
     x1_sem, loc_sem, halo_s, halo_r, c_s, c_r, r_s, r_r, y_s, y_r, z_s, z_r, st_s, st_r,
 ):
     seq = lax.axis_index("seq")
@@ -68,6 +68,7 @@
     peers = [(sid(y, x, 1 - c), z), (lax.rem(seq + 2 * c + 31, 32), z)]
     peers += [(plane(o), z) for o in range(1, NX * NY)]
     peers += [(seq, lax.rem(z + o, NZ)) for o in range(1, NZ)]
+    peers += [(sid(y, x, 1 - c), lax.rem(z + o, NZ)) for o in range(1, NZ)]
     for s, zz in peers:
         pl.semaphore_signal(bar, inc=1, device_id={"seq": s, "dp": zz}, device_id_type=MESH)
     pl.semaphore_wait(bar, len(peers))
@@ -157,7 +158,7 @@
         to = along_z[o]
         return rdma(zs.at[l, g, to], zr.at[l, g, o - 1], z_s.at[l, g, o - 1], z_r.at[l, g, o - 1], to_z=to)
 
-    def stage_a(l, u, beside=None):
+    def stage_a(l, u, *beside):
         d = DIL[l]
         t = kind(l, u)
         off = pl.multiple_of(lax.rem(lax.div(u, 3) + 1, 3) * d, 16)
@@ -165,14 +166,16 @@
         rhs = cots[l][:, pl.ds(off, B), pl.ds(n0, 256)].reshape(W * B, 256)
         csend[l, u] = jnp.dot(ats[l][t, 1 - c], rhs, preferred_element_type=F32).astype(BF16)
         keep[l, u] = jnp.dot(ats[l][t, c], rhs, preferred_element_type=F32)
-        if beside is not None:
-            beside()
+        for also in beside:
+            also()
         core_copy(l, u).start()
 
-    def stage_b(l, u):
+    def b_wait(l, u):
+        core_copy(l, u).wait_recv()
+
+    def b_work(l, u):
         t = kind(l, u)
         p = jnp.where(t == 0, x, y)
-        core_copy(l, u).wait_recv()
 
         def rows(o):
             return pl.ds(pl.multiple_of(lax.rem(p + o, 4) * ROWS, 16), ROWS)
@@ -183,8 +186,16 @@
 
         for o in (2, 1, 3):
             rsend[l, u, o - 1] = total(o).astype(BF16)
+        keep[l, u, rows(0), :] = total(0)
+
+    def b_send(l, u):
+        for o in (2, 1, 3):
             ring_copy(l, u, o).start()
-        keep[l, u, rows(0), :] = total(0)
+
+    def stage_b(l, u):
+        b_wait(l, u)
+        b_work(l, u)
+        b_send(l, u)
 
     def stage_d(l, u):
         t = kind(l, u)
@@ -202,12 +213,18 @@
             far_copy(l, u, o).start()
         yown[u] = tbuf[q]
 
-    def stage_e(l, u):
+    def e_wait(l, u):
         for o in (1, 3, 2):
             far_copy(l, u, o).wait_recv()
+
+    def e_work(l, u):
         n0 = pl.multiple_of(lax.rem(u, 3) * 256, 256)
         s = yrecv[l, u, 0].astype(F32) + yrecv[l, u, 1].astype(F32) + yrecv[l, u, 2].astype(F32)
         zb[tap_of(u), :, pl.ds(n0, 256)] = yown[u] + jnp.concatenate([s[:24], s[24:]], axis=1)
+
+    def stage_e(l, u):
+        e_wait(l, u)
+        e_work(l, u)
 
     def stage_z(l, g):
         v = zb[TAPS[g]]
@@ -264,30 +281,28 @@
                 else:
                     gin[w, r, :] = (run[w, r, :] + dx).astype(BF16)
 
-    bufs = (sa0, sa1, sa2)
-    places = (c, y * NX + x, z)
-    counts = (2, NX * NY, NZ)
-    first = (0, 1, NX * NY)
+    bufs = (sa0, sa1)
+    places = (z * 2 + c, y * NX + x)
+    counts = (2 * NZ, NX * NY)
 
     def stat_copy(e, ax, o, sending):
         lo, cnt = ((0, 1), (1, 3))[e]
         if ax == 0:
-            to, back = dict(to_seq=sid(y, x, 1 - c)), 1 - c
-        elif ax == 1:
+            flip, on = o % 2, o // 2
+            to = dict(to_seq=twin if flip else seq, to_z=along_z[on])
+            back = lax.rem(z + NZ - on, NZ) * 2 + (1 - c if flip else c)
+        else:
             to = dict(to_seq=plane(o))
             back = lax.rem(y + NY - o // NX, NY) * NX + lax.rem(x + NX - o % NX, NX)
-        else:
-            to, back = dict(to_z=lax.rem(z + o, NZ)), lax.rem(z + NZ - o, NZ)
         ref = bufs[ax].at[places[ax] if sending else back, pl.ds(lo, cnt)]
-        i = first[ax] + o - 1
-        return rdma(ref, ref, st_s.at[e, i], st_r.at[e, i], **to)
+        return rdma(ref, ref, st_s.at[e, ax, o - 1], st_r.at[e, ax, o - 1], **to)
 
     def stat_put(e):
         for i in ((0,), (1, 2, 3))[e]:
             v = jnp.sum(sacc[i], axis=0, keepdims=True)
-            sa0[c, i] = jnp.zeros((8, 128), F32)
+            sa0[places[0], i] = jnp.zeros((8, 128), F32)
             for j in range(6):
-                sa0[c, i, j : j + 1, :] = v[:, j * 128 : j * 128 + 128]
+                sa0[places[0], i, j : j + 1, :] = v[:, j * 128 : j * 128 + 128]
 
     def stat_send(e, ax):
         for o in range(1, counts[ax]):
@@ -300,7 +315,7 @@
         tot = bufs[ax][0, lo : lo + cnt]
         for i in range(1, counts[ax]):
             tot = tot + bufs[ax][i, lo : lo + cnt]
-        if ax < 2:
+        if ax < 1:
             bufs[ax + 1][places[ax + 1], lo : lo + cnt] = tot
         else:
             tot = tot * SCALE
@@ -326,16 +341,25 @@
     def _(u):
         stage_a(1, u, lambda: forward(0, u))
 
+    stage_b(1, 0)
+    stage_b(1, 1)
     for h in halo1():
         h.wait_recv()
     clear_ends(1)
 
-    @pl.loop(3, 6)
+    @pl.loop(3, 8)
     def _(u):
         stage_a(1, u, lambda: forward(0, u))
-        stage_b(1, u - 3)
-
+        stage_b(1, u - 1)
+
+    stage_a(1, 8)
+    stage_b(1, 7)
     ld_w[1].wait()
+
+    def thrice(stage, l, lo):
+        @pl.loop(lo, lo + 3)
+        def _(u):
+            stage(l, u)
 
     @pl.loop(0, 4)
     def _(m):
@@ -344,34 +368,26 @@
         for h in halo0(m):
             h.start()
 
-        @pl.loop(0, 3)
-        def _(i):
-            @pl.when(m == 0)
-            def _():
-                stage_b(1, 3 + i)
-
-            @pl.when(m == 3)
-            def _():
-                stage_d(1, i)
+        @pl.when(m == 0)
+        def _():
+            stage_b(1, 8)
+
+        @pl.when(m == 3)
+        def _():
+            thrice(stage_d, 1, 0)
 
     stat_put(1)
     stat_send(1, 0)
-
-    @pl.loop(6, 8)
-    def _(u):
-        stage_a(1, u, lambda: forward(0, u))
-        stage_d(1, u - 3)
-
-    stage_a(1, 8)
-    stage_d(1, 5)
 
     @pl.loop(0, 3)
     def _(u):
         stage_a(0, u)
-        stage_b(1, 6 + u)
+        stage_d(1, 3 + u)
 
     stat_recv(1, 0)
     stat_send(1, 1)
+    stage_b(0, 0)
+    stage_b(0, 1)
     for m in range(4):
         for h in halo0(m):
             h.wait_recv()
@@ -379,10 +395,11 @@
 
     @pl.loop(3, UNITS)
     def _(u):
-        stage_a(0, u)
-        stage_b(0, u - 3)
-        stage_e(1, u - 3)
-
+        e_wait(1, u - 3)
+        stage_a(0, u, lambda: e_work(1, u - 3))
+        stage_b(0, u - 1)
+
+    stage_b(0, 8)
     stage_z(1, 0)
     stage_z(1, 1)
     ld_w[0].wait()
@@ -392,38 +409,28 @@
         matmul(0, m)
         backward(0, m)
 
-        @pl.loop(0, 3)
-        def _(i):
-            @pl.when(m == 0)
-            def _():
-                stage_b(0, 6 + i)
-
-            @pl.when(m == 1)
-            def _():
-                stage_d(1, 6 + i)
-
-            @pl.when(m == 2)
-            def _():
-                stage_d(0, i)
-
-            @pl.when(m == 3)
-            def _():
-                stage_e(1, 6 + i)
-
+        @pl.when(m == 0)
+        def _():
+            thrice(stage_d, 1, 6)
+
+        @pl.when(m == 2)
+        def _():
+            thrice(stage_e, 1, 6)
+
+        @pl.when(m == 3)
+        def _():
+            thrice(stage_d, 0, 0)
+
+    stage_z(1, 2)
     stat_put(0)
     stat_send(0, 0)
-    stat_recv(1, 1)
-    stat_send(1, 2)
-    stat_recv(0, 0)
-    stat_send(0, 1)
-    stage_z(1, 2)
 
     @pl.loop(3, UNITS)
     def _(u):
         stage_d(0, u)
 
-    stat_recv(0, 1)
-    stat_send(0, 2)
+    stat_recv(0, 0)
+    stat_send(0, 1)
     for g in range(3):
 
         @pl.loop(3 * g, 3 * g + 3)
@@ -434,9 +441,9 @@
         if g == 0:
             for k in range(3):
                 stage_last(1, k)
-            stat_recv(1, 2)
-
-    stat_recv(0, 2)
+            stat_recv(1, 1)
+
+    stat_recv(0, 1)
     for g in range(3):
         stage_last(0, g)
 
@@ -462,7 +469,7 @@
             for o in range(1, NZ):
                 z_copy(l, g, o).wait_send()
     for e in range(2):
-        for ax in range(3):
+        for ax in range(2):
             for o in range(1, counts[ax]):
                 stat_copy(e, ax, o, True).wait_send()
 
@@ -498,9 +505,8 @@
         zr=vm((2, 3, NZ - 1, 32, 128), BF16),
         zown=vm((2, 3, 24, 128), F32),
         sacc=vm((4, 8, C), F32),
-        sa0=vm((2, 4, 8, 128), F32),
+        sa0=vm((2 * NZ, 4, 8, 128), F32),
         sa1=vm((NX * NY, 4, 8, 128), F32),
-        sa2=vm((NZ, 4, 8, 128), F32),
         x1_sem=dma((W,)),
         loc_sem=dma((5,)),
         halo_s=dma((10,)),
@@ -513,8 +519,8 @@
         y_r=dma((2, UNITS, 3)),
         z_s=dma((2, 3, NZ - 1)),
         z_r=dma((2, 3, NZ - 1)),
-        st_s=dma((2, 23)),
-        st_r=dma((2, 23)),
+        st_s=dma((2, 2, 15)),
+        st_r=dma((2, 2, 15)),
     )
     names = list(scratch)
 

time: 69.5 us -> 76.8 us (1.11)
  Pallas kernels: 66.3 us -> 73.7 us
    pallas_call x1, Pallas kernels: 66.3 us -> 73.7 us  [local(): pl.pallas_call(kernel, out_shape=(vm((W, B, C), BF16), vm((2, 3, 24, 96),...]
where the time goes in v5:
time: 76.8 us; the launch traced here: 76.7 us
  Pallas kernels  73.7 us (96%)
  local copies, waits for them, and re-layouts  2.38 us (3%)
    pallas_call x1, Pallas kernels, local(): pl.pallas_call(kernel, out_shape=(vm((W, B, C), BF16), vm((2, 3, 24, 96),...  73.7 us
    unnamed x3, local copies, waits for them, and re-layouts  2.38 us

profile of v5, /device:TPU:1, one launch (start us, length us, event | category | flops | bytes accessed | tf_op | source)
XLA Modules:
  0.0 76.7 jit_solution(4059826044741979016)
XLA Ops:
  0.6 73.7 %shard_map.67 = (bf16[8,128,768]{2,1,0:T(8,128)(2,1)S(1)}, f32[2,3,24,96]{3,2,1,0:T(8,128)S(1)}, f32[2,2,768]{2,1,0:T(2,128)S(1)}) custom-call(bf16[2,8,128,768]{3,2,1,0:T(8,128)(2,1)} %refs_0_.1, bf16[8,128,768]{2,1,0:T(8,128)(2,1)} %refs_1_.1, f32[2,768]{1,0:T(2,128)} %refs_2_.1, bf16[2,3,768,768]{3,2,1,0:T(8,128)(2,1)} %bitcast.3), custom_call_target="tpu_custom_call" | custom-call | flops 14499999744 | bytes 13000000 | tf_op jit(solution)/shard_map/pallas_call | solution.py:531
  74.3 1.1 %copy.10 = bf16[8,128,768]{2,1,0:T(8,128)(2,1)} copy(bf16[8,128,768]{2,1,0:T(8,128)(2,1)S(1)} %get-tuple-element.9) | data formatting | bytes 3145728
  75.5 0.6 copy.11
  76.1 0.6 copy.12

commit v6 on v5

--- a/solution.py
+++ b/solution.py
@@ -341,19 +341,16 @@
     def _(u):
         stage_a(1, u, lambda: forward(0, u))
 
-    stage_b(1, 0)
-    stage_b(1, 1)
     for h in halo1():
         h.wait_recv()
     clear_ends(1)
 
-    @pl.loop(3, 8)
+    @pl.loop(3, 6)
     def _(u):
-        stage_a(1, u, lambda: forward(0, u))
-        stage_b(1, u - 1)
-
-    stage_a(1, 8)
-    stage_b(1, 7)
+        b_wait(1, u - 3)
+        stage_a(1, u, lambda: forward(0, u), lambda: b_work(1, u - 3))
+        b_send(1, u - 3)
+
     ld_w[1].wait()
 
     def thrice(stage, l, lo):
@@ -370,7 +367,7 @@
 
         @pl.when(m == 0)
         def _():
-            stage_b(1, 8)
+            thrice(stage_b, 1, 3)
 
         @pl.when(m == 3)
         def _():
@@ -379,15 +376,22 @@
     stat_put(1)
     stat_send(1, 0)
 
+    @pl.loop(6, 8)
+    def _(u):
+        stage_a(1, u, lambda: forward(0, u))
+        stage_d(1, u - 3)
+
+    stage_a(1, 8)
+    stage_d(1, 5)
+
     @pl.loop(0, 3)
     def _(u):
-        stage_a(0, u)
-        stage_d(1, 3 + u)
+        b_wait(1, 6 + u)
+        stage_a(0, u, lambda: b_work(1, 6 + u))
+        b_send(1, 6 + u)
 
     stat_recv(1, 0)
     stat_send(1, 1)
-    stage_b(0, 0)
-    stage_b(0, 1)
     for m in range(4):
         for h in halo0(m):
             h.wait_recv()
@@ -396,12 +400,15 @@
     @pl.loop(3, UNITS)
     def _(u):
         e_wait(1, u - 3)
-        stage_a(0, u, lambda: e_work(1, u - 3))
-        stage_b(0, u - 1)
-
+        b_wait(0, u - 3)
+        stage_a(0, u, lambda: b_work(0, u - 3), lambda: e_work(1, u - 3))
+        b_send(0, u - 3)
+
+    stage_b(0, 6)
+    stage_z(1, 0)
+    stage_b(0, 7)
+    stage_z(1, 1)
     stage_b(0, 8)
-    stage_z(1, 0)
-    stage_z(1, 1)
     ld_w[0].wait()
 
     @pl.loop(0, 4)
@@ -409,28 +416,26 @@
         matmul(0, m)
         backward(0, m)
 
-        @pl.when(m == 0)
+        @pl.when(m == 1)
         def _():
             thrice(stage_d, 1, 6)
 
         @pl.when(m == 2)
         def _():
+            thrice(stage_d, 0, 0)
+
+        @pl.when(m == 3)
+        def _():
             thrice(stage_e, 1, 6)
-
-        @pl.when(m == 3)
-        def _():
-            thrice(stage_d, 0, 0)
 
     stage_z(1, 2)
     stat_put(0)
     stat_send(0, 0)
 
-    @pl.loop(3, UNITS)
-    def _(u):
-        stage_d(0, u)
-
+    thrice(stage_d, 0, 3)
     stat_recv(0, 0)
     stat_send(0, 1)
+    thrice(stage_d, 0, 6)
     for g in range(3):
 
         @pl.loop(3 * g, 3 * g + 3)

time: 76.8 us -> 73.4 us (0.956)
  Pallas kernels: 73.7 us -> 70.3 us
    pallas_call x1, Pallas kernels: 73.7 us -> 70.3 us  [local(): pl.pallas_call(kernel, out_shape=(vm((W, B, C), BF16), vm((2, 3, 24, 96),...]
where the time goes in v6:
time: 73.4 us; the launch traced here: 73.3 us
  Pallas kernels  70.3 us (96%)
  local copies, waits for them, and re-layouts  2.38 us (3%)
    pallas_call x1, Pallas kernels, local(): pl.pallas_call(kernel, out_shape=(vm((W, B, C), BF16), vm((2, 3, 24, 96),...  70.3 us
    unnamed x3, local copies, waits for them, and re-layouts  2.38 us

profile of v6, /device:TPU:1, one launch (start us, length us, event | category | flops | bytes accessed | tf_op | source)
XLA Modules:
  0.0 73.3 jit_solution(2794672574569557352)
XLA Ops:
  0.6 70.3 %shard_map.67 = (bf16[8,128,768]{2,1,0:T(8,128)(2,1)S(1)}, f32[2,3,24,96]{3,2,1,0:T(8,128)S(1)}, f32[2,2,768]{2,1,0:T(2,128)S(1)}) custom-call(bf16[2,8,128,768]{3,2,1,0:T(8,128)(2,1)} %refs_0_.1, bf16[8,128,768]{2,1,0:T(8,128)(2,1)} %refs_1_.1, f32[2,768]{1,0:T(2,128)} %refs_2_.1, bf16[2,3,768,768]{3,2,1,0:T(8,128)(2,1)} %bitcast.3), custom_call_target="tpu_custom_call" | custom-call | flops 14499999744 | bytes 13000000 | tf_op jit(solution)/shard_map/pallas_call | solution.py:536
  70.9 1.1 %copy.10 = bf16[8,128,768]{2,1,0:T(8,128)(2,1)} copy(bf16[8,128,768]{2,1,0:T(8,128)(2,1)S(1)} %get-tuple-element.9) | data formatting | bytes 3145728
  72.1 0.6 copy.11
  72.7 0.6 copy.12

commit v7 on v4

--- a/solution.py
+++ b/solution.py
@@ -377,11 +377,16 @@
             h.wait_recv()
     clear_ends(0)
 
-    @pl.loop(3, UNITS)
+    stage_a(0, 3)
+    stage_e(1, 0)
+
+    @pl.loop(4, UNITS)
     def _(u):
         stage_a(0, u)
-        stage_b(0, u - 3)
+        stage_b(0, u - 4)
         stage_e(1, u - 3)
+
+    stage_b(0, 5)
 
     stage_z(1, 0)
     stage_z(1, 1)

time: 69.5 us -> 69.4 us (level)
  no operation moved by 1% of the time
where the time goes in v7:
time: 69.4 us; the launch traced here: 69.2 us
  Pallas kernels  66.2 us (95%)
  local copies, waits for them, and re-layouts  2.38 us (3%)
    pallas_call x1, Pallas kernels, local(): pl.pallas_call(kernel, out_shape=(vm((W, B, C), BF16), vm((2, 3, 24, 96),...  66.2 us
    unnamed x3, local copies, waits for them, and re-layouts  2.38 us

profile of v7, /device:TPU:1, one launch (start us, length us, event | category | flops | bytes accessed | tf_op | source)
XLA Modules:
  0.0 69.2 jit_solution(4645643361101397381)
XLA Ops:
  0.6 66.2 %shard_map.67 = (bf16[8,128,768]{2,1,0:T(8,128)(2,1)S(1)}, f32[2,3,24,96]{3,2,1,0:T(8,128)S(1)}, f32[2,2,768]{2,1,0:T(2,128)S(1)}) custom-call(bf16[2,8,128,768]{3,2,1,0:T(8,128)(2,1)} %refs_0_.1, bf16[8,128,768]{2,1,0:T(8,128)(2,1)} %refs_1_.1, f32[2,768]{1,0:T(2,128)} %refs_2_.1, bf16[2,3,768,768]{3,2,1,0:T(8,128)(2,1)} %bitcast.3), custom_call_target="tpu_custom_call" | custom-call | flops 14499999744 | bytes 13000000 | tf_op jit(solution)/shard_map/pallas_call | solution.py:530
  66.9 1.1 %copy.10 = bf16[8,128,768]{2,1,0:T(8,128)(2,1)} copy(bf16[8,128,768]{2,1,0:T(8,128)(2,1)S(1)} %get-tuple-element.9) | data formatting | bytes 3145728
  68.0 0.6 copy.11
  68.6 0.6 copy.12
